TPU v7x, 512 devices: a whole 4x8x8 slice. The times are simulated.
512 devices in a mesh: segment: 16 (over y, core), expert: 32 (over x, z).
Axes of the slice: x: 4, y: 8, z: 8, core: 2. Of those that a mesh axis runs over, the one named last changes fastest.
Arguments:
- state: bfloat16 [16, 256, 2048], P('segment', 'expert'), may hold values from -24 to 24
- routes: int32 [4, 16, 256, 2], P(None, 'segment', 'expert'), may hold values from 0 to 3, all different within a row; in each aligned block of 8 rows (0 to 7, 8 to 15, ..., all dimensions but the last counted through in order) at most 6 rows name the same one
- gates: float32 [4, 16, 256, 2], P(None, 'segment', 'expert'), may hold values from 0.2 to 1
- norm_gain: float32 [2, 16, 2048], P(None, 'segment'), may hold values from 0.25 to 1.75
- w_gate: bfloat16 [2, 16, 5120, 2048], P(None, 'segment', 'expert'), may hold values from -0.125 to 0.125
- w_up: bfloat16 [2, 16, 5120, 2048], P(None, 'segment', 'expert'), may hold values from -0.125 to 0.125
- w_down: bfloat16 [2, 16, 5120, 2048], P(None, 'segment', 'expert'), may hold values from -0.15625 to 0.15625
- spare_gate: bfloat16 [2, 16, 1280, 2048], P(None, 'segment', 'expert'), may hold values from -0.125 to 0.125
- spare_up: bfloat16 [2, 16, 1280, 2048], P(None, 'segment', 'expert'), may hold values from -0.125 to 0.125
- spare_down: bfloat16 [2, 16, 1280, 2048], P(None, 'segment', 'expert'), may hold values from -0.15625 to 0.15625
Outputs:
- final: bfloat16 [16, 256, 2048], P('segment', 'expert')
Inputs may be any that keep to these rules, and one draw needn't show every extreme that they name: `routes`: each row names 2 different experts. Within the 8 rows of one device at one tick (aligned blocks), no expert is named by more than 6 rows, and some blocks reach 6.
All inputs are finite; a program needn't handle non-finite values.
Results may differ from a plain program's by a relative error of at most 0.012.
Values may be sent and summed in bfloat16 or wider, within the bound.
A program may use at most 64 MiB of HBM per device.

v0:
```python
import jax
import jax.numpy as jnp
from jax import lax
from jax.sharding import PartitionSpec as P

EXPERTS = 4
TICKS = 4
CAP = 4


EPSILON = 1e-06


def laid_out(pieces, dim):
    pieces = jnp.moveaxis(pieces, 0, dim)
    shape = pieces.shape
    return pieces.reshape(*shape[:dim], shape[dim] * shape[dim + 1], *shape[dim + 2 :])


def sent_to_all(shard, axis):
    peers = lax.axis_size(axis)
    return lax.all_to_all(
        jnp.broadcast_to(shard[None], (peers, *shard.shape)), axis, 0, 0, tiled=True
    )


def gathered_copies(shard, axis, dim):
    return laid_out(sent_to_all(shard, axis), dim)


def from_behind(value, axis, steps):
    count = lax.axis_size(axis)
    pairs = [(source, (source + steps) % count) for source in range(count)]
    return lax.ppermute(value, axis, pairs)


def rms_normed(rows, norm_scale):
    values = rows.astype(jnp.float32)
    row_scale = lax.rsqrt(jnp.mean(values * values, axis=-1, keepdims=True) + EPSILON)
    return (values * row_scale * norm_scale).astype(jnp.bfloat16)


def expert_rows(rows, gate_block, up_block, down_block):
    contract = (((1,), (1,)), ((), ()))
    gate_pre = lax.dot_general(rows, gate_block, contract, preferred_element_type=jnp.float32)
    up_pre = lax.dot_general(rows, up_block, contract, preferred_element_type=jnp.float32)
    hidden = (jax.nn.silu(gate_pre) * up_pre).astype(jnp.bfloat16)
    return jnp.dot(hidden, down_block, preferred_element_type=jnp.float32).astype(jnp.bfloat16)


def group_of(section, tick_idx, segments):
    start_segment = (section - tick_idx) % segments
    first_group = jnp.where((start_segment % 2 == 1) & (start_segment + TICKS <= segments), 1, 0)
    return (first_group + jnp.where(start_segment + tick_idx >= segments, 1, 0)).astype(jnp.int32)


def spare_served(rows, gate_block, up_block, down_block):
    members = lax.axis_size("expert")
    tok_dev = rows.shape[0]
    model_width = rows.shape[1]
    gathered = expert_rows(gathered_copies(rows, "expert", 0), gate_block, up_block, down_block)
    returned = lax.all_to_all(
        gathered.reshape(members, tok_dev, model_width),
        "expert",
        split_axis=0,
        concat_axis=0,
        tiled=True,
    )
    return jnp.sum(returned.astype(jnp.float32), axis=0)


def on_device(
    state, routes, gates, norm_gain, w_gate, w_up, w_down, spare_gate, spare_up, spare_down
):
    segments = lax.axis_size("segment")
    segment_idx = lax.axis_index("segment")
    members = lax.axis_size("expert")
    split_count = members // EXPERTS
    tok_dev = state.shape[1]
    model_width = state.shape[2]
    current = state[0]
    labels = jnp.arange(EXPERTS, dtype=jnp.int32)
    for tick_idx in range(TICKS):
        group_idx = group_of(segment_idx, tick_idx, segments)
        spare_group = group_of(segment_idx + segments - 1, tick_idx, segments)
        norm_scale = lax.dynamic_index_in_dim(norm_gain[:, 0], group_idx, 0, keepdims=False)
        gate_block = lax.dynamic_index_in_dim(w_gate[:, 0], group_idx, 0, keepdims=False)
        up_block = lax.dynamic_index_in_dim(w_up[:, 0], group_idx, 0, keepdims=False)
        down_block = lax.dynamic_index_in_dim(w_down[:, 0], group_idx, 0, keepdims=False)
        spare_g = lax.dynamic_index_in_dim(spare_gate[:, 0], spare_group, 0, keepdims=False)
        spare_u = lax.dynamic_index_in_dim(spare_up[:, 0], spare_group, 0, keepdims=False)
        spare_d = lax.dynamic_index_in_dim(spare_down[:, 0], spare_group, 0, keepdims=False)
        normed = rms_normed(current, norm_scale)
        chosen = routes[tick_idx, 0]
        weights = gates[tick_idx, 0]
        matches = chosen[:, :, None] == labels[None, None, :]
        routed = jnp.sum(jnp.where(matches, weights[:, :, None], jnp.float32(0.0)), axis=1)
        member_of = jnp.any(matches, axis=1)
        taken = member_of.astype(jnp.int32)
        position = jnp.cumsum(taken, axis=0, dtype=jnp.int32) - taken
        inside = member_of & (position < CAP)
        spill = jnp.sum(jnp.where(inside, jnp.float32(0.0), routed), axis=1)
        slot_ids = jnp.arange(CAP, dtype=jnp.int32)
        select = inside[:, :, None] & (position[:, :, None] == slot_ids[None, None, :])
        picker = select.astype(jnp.bfloat16)
        outgoing = jnp.einsum(
            "tej,td->ejd", picker, normed, preferred_element_type=jnp.float32
        ).astype(jnp.bfloat16)
        outgoing = jnp.repeat(outgoing, split_count, axis=0)
        arrived = lax.all_to_all(outgoing, "expert", split_axis=0, concat_axis=0, tiled=True)
        slot_count = arrived.shape[1]
        partial_value = expert_rows(
            arrived.reshape(-1, model_width), gate_block, up_block, down_block
        )
        returned = lax.all_to_all(
            partial_value.reshape(members, slot_count, model_width),
            "expert",
            split_axis=0,
            concat_axis=0,
            tiled=True,
        )
        coefficient = jnp.where(select, routed[:, :, None], jnp.float32(0.0))
        coefficient = jnp.repeat(coefficient, split_count, axis=1).reshape(tok_dev, members * CAP)
        combined = jnp.dot(
            coefficient, returned.reshape(members * CAP, model_width).astype(jnp.float32)
        )
        stacked = jnp.stack([spare_g, spare_u, spare_d])
        fetched = from_behind(stacked, "segment", -1)
        spare_out = spare_served(normed, fetched[0], fetched[1], fetched[2])
        combined = combined + spill[:, None] * spare_out
        current = (current.astype(jnp.float32) + combined).astype(jnp.bfloat16)
        if tick_idx + 1 < TICKS:
            current = from_behind(current, "segment", 1)
    return current[None]


def solution(mesh):
    return jax.shard_map(
        on_device,
        mesh=mesh,
        in_specs=(
            P("segment", "expert", None),
            P(None, "segment", "expert", None),
            P(None, "segment", "expert", None),
            P(None, "segment", None),
            P(None, "segment", "expert", None),
            P(None, "segment", "expert", None),
            P(None, "segment", "expert", None),
            P(None, "segment", "expert", None),
            P(None, "segment", "expert", None),
            P(None, "segment", "expert", None),
        ),
        out_specs=P("segment", "expert", None),
        check_vma=False,
    )
```

profile of v0, /device:TPU:1, one launch (start us, length us, event | category | flops | bytes accessed | tf_op | source)
XLA Modules:
  0.0 472.7 jit_solution(11733261014145943397)
XLA Ops:
  7.3 13.7 %all-to-all-start = ((bf16[32,4,2048]{2,1,0:T(4,128)(2,1)}), bf16[32,4,2048]{2,1,0:T(4,128)(2,1)S(1)}, u32[]{:S(2)}, u32[]{:S(2)}) async-start(bf16[32,4,2048]{2,1,0:T(4,128)(2,1)} %bitcast.6), calls=%async_computation | async-start | bytes 1048576 | tf_op jit(solution)/shard_map/all_to_all | solution.py:110
  21.1 14.2 %all-to-all-done = bf16[32,4,2048]{2,1,0:T(4,128)(2,1)S(1)} async-done(((bf16[32,4,2048]{2,1,0:T(4,128)(2,1)}), bf16[32,4,2048]{2,1,0:T(4,128)(2,1)S(1)}, u32[]{:S(2)}, u32[]{:S(2)}) %all-to-all-start) | async-done | bytes 524320 | tf_op jit(solution)/shard_map/all_to_all | solution.py:110
  52.1 16.6 %all-to-all-done.2 = bf16[32,8,2048]{2,1,0:T(8,128)(2,1)S(1)} async-done(((bf16[32,8,2048]{2,1,0:T(8,128)(2,1)}), bf16[32,8,2048]{2,1,0:T(8,128)(2,1)S(1)}, u32[]{:S(2)}, u32[]{:S(2)}) %all-to-all-start.2) | async-done | bytes 1048608 | tf_op jit(solution)/shard_map/all_to_all | solution.py:22
  68.7 8.5 %all-to-all-start.1 = ((bf16[32,4,2048]{2,1,0:T(4,128)(2,1)}), bf16[32,4,2048]{2,1,0:T(4,128)(2,1)S(1)}, u32[]{:S(2)}, u32[]{:S(2)}) async-start(bf16[32,4,2048]{2,1,0:T(4,128)(2,1)} %reshape.232), calls=%async_computation.1 | async-start | bytes 1048576 | tf_op jit(solution)/shard_map/all_to_all | solution.py:115
  79.9 8.0 %collective-permute-done = bf16[3,40,2048]{2,1,0:T(8,128)(2,1)S(1)} collective-permute-done((bf16[3,40,2048]{2,1,0:T(8,128)(2,1)S(1)}, bf16[3,40,2048]{2,1,0:T(8,128)(2,1)S(1)}, u32[]{:S(2)}, u32[]{:S(2)}) %collective-permute-start) | collective-permute-done | bytes 491552 | tf_op jit(solution)/shard_map/ppermute | solution.py:34
  91.0 9.2 %all-to-all-start.3 = ((bf16[32,8,2048]{2,1,0:T(8,128)(2,1)}), bf16[32,8,2048]{2,1,0:T(8,128)(2,1)S(1)}, u32[]{:S(2)}, u32[]{:S(2)}) async-start(bf16[32,8,2048]{2,1,0:T(8,128)(2,1)} %fusion), calls=%async_computation.3 | async-start | bytes 2097152 | tf_op jit(solution)/shard_map/all_to_all | solution.py:62
  101.1 24.2 %all-to-all-done.3 = bf16[32,8,2048]{2,1,0:T(8,128)(2,1)S(1)} async-done(((bf16[32,8,2048]{2,1,0:T(8,128)(2,1)}), bf16[32,8,2048]{2,1,0:T(8,128)(2,1)S(1)}, u32[]{:S(2)}, u32[]{:S(2)}) %all-to-all-start.3) | async-done | bytes 1048608 | tf_op jit(solution)/shard_map/all_to_all | solution.py:62
  133.0 17.0 %all_to_all.80 = bf16[32,4,2048]{2,1,0:T(4,128)(2,1)S(1)} all-to-all(bf16[32,4,2048]{2,1,0:T(4,128)(2,1)S(1)} %bitcast.237), channel_id=1, replica_groups=mesh['segment'=16,'expert'=32] {'expert'}, dimensions={0} | all-to-all | bytes 1048576 | tf_op jit(solution)/shard_map/all_to_all | solution.py:110
  151.1 7.7 %all-to-all-start.6 = ((bf16[32,8,2048]{2,1,0:T(8,128)(2,1)}), bf16[32,8,2048]{2,1,0:T(8,128)(2,1)S(1)}, u32[]{:S(2)}, u32[]{:S(2)}) async-start(bf16[32,8,2048]{2,1,0:T(8,128)(2,1)} %broadcast_in_dim.175), calls=%async_computation.6 | async-start | bytes 2097152 | tf_op jit(solution)/shard_map/all_to_all | solution.py:22
  163.4 16.9 %all-to-all-done.6 = bf16[32,8,2048]{2,1,0:T(8,128)(2,1)S(1)} async-done(((bf16[32,8,2048]{2,1,0:T(8,128)(2,1)}), bf16[32,8,2048]{2,1,0:T(8,128)(2,1)S(1)}, u32[]{:S(2)}, u32[]{:S(2)}) %all-to-all-start.6) | async-done | bytes 1048608 | tf_op jit(solution)/shard_map/all_to_all | solution.py:22
  180.3 9.1 %all-to-all-start.5 = ((bf16[32,4,2048]{2,1,0:T(4,128)(2,1)}), bf16[32,4,2048]{2,1,0:T(4,128)(2,1)S(1)}, u32[]{:S(2)}, u32[]{:S(2)}) async-start(bf16[32,4,2048]{2,1,0:T(4,128)(2,1)} %reshape.238), calls=%async_computation.5 | async-start | bytes 1048576 | tf_op jit(solution)/shard_map/all_to_all | solution.py:115
  194.7 9.7 %collective-permute-done.2 = bf16[3,40,2048]{2,1,0:T(8,128)(2,1)S(1)} collective-permute-done((bf16[3,40,2048]{2,1,0:T(8,128)(2,1)S(1)}, bf16[3,40,2048]{2,1,0:T(8,128)(2,1)S(1)}, u32[]{:S(2)}, u32[]{:S(2)}) %collective-permute-start.2) | collective-permute-done | bytes 491552 | tf_op jit(solution)/shard_map/ppermute | solution.py:34
  207.2 9.2 %all-to-all-start.7 = ((bf16[32,8,2048]{2,1,0:T(8,128)(2,1)}), bf16[32,8,2048]{2,1,0:T(8,128)(2,1)S(1)}, u32[]{:S(2)}, u32[]{:S(2)}) async-start(bf16[32,8,2048]{2,1,0:T(8,128)(2,1)} %fusion.1), calls=%async_computation.7 | async-start | bytes 2097152 | tf_op jit(solution)/shard_map/all_to_all | solution.py:62
  217.7 25.6 %all-to-all-done.7 = bf16[32,8,2048]{2,1,0:T(8,128)(2,1)S(1)} async-done(((bf16[32,8,2048]{2,1,0:T(8,128)(2,1)}), bf16[32,8,2048]{2,1,0:T(8,128)(2,1)S(1)}, u32[]{:S(2)}, u32[]{:S(2)}) %all-to-all-start.7) | async-done | bytes 1048608 | tf_op jit(solution)/shard_map/all_to_all | solution.py:62
  249.4 21.9 %all_to_all.81 = bf16[32,4,2048]{2,1,0:T(4,128)(2,1)S(1)} all-to-all(bf16[32,4,2048]{2,1,0:T(4,128)(2,1)S(1)} %bitcast.238), channel_id=1, replica_groups=mesh['segment'=16,'expert'=32] {'expert'}, dimensions={0} | all-to-all | bytes 1048576 | tf_op jit(solution)/shard_map/all_to_all | solution.py:110
  282.7 21.2 %all-to-all-done.10 = bf16[32,8,2048]{2,1,0:T(8,128)(2,1)S(1)} async-done(((bf16[32,8,2048]{2,1,0:T(8,128)(2,1)}), bf16[32,8,2048]{2,1,0:T(8,128)(2,1)S(1)}, u32[]{:S(2)}, u32[]{:S(2)}) %all-to-all-start.10) | async-done | bytes 1048608 | tf_op jit(solution)/shard_map/all_to_all | solution.py:22
  303.8 7.9 %all-to-all-start.9 = ((bf16[32,4,2048]{2,1,0:T(4,128)(2,1)}), bf16[32,4,2048]{2,1,0:T(4,128)(2,1)S(1)}, u32[]{:S(2)}, u32[]{:S(2)}) async-start(bf16[32,4,2048]{2,1,0:T(4,128)(2,1)} %reshape.244), calls=%async_computation.9 | async-start | bytes 1048576 | tf_op jit(solution)/shard_map/all_to_all | solution.py:115
  325.8 7.8 %all-to-all-start.11 = ((bf16[32,8,2048]{2,1,0:T(8,128)(2,1)}), bf16[32,8,2048]{2,1,0:T(8,128)(2,1)S(1)}, u32[]{:S(2)}, u32[]{:S(2)}) async-start(bf16[32,8,2048]{2,1,0:T(8,128)(2,1)} %fusion.2), calls=%async_computation.11 | async-start | bytes 2097152 | tf_op jit(solution)/shard_map/all_to_all | solution.py:62
  334.5 23.7 %all-to-all-done.11 = bf16[32,8,2048]{2,1,0:T(8,128)(2,1)S(1)} async-done(((bf16[32,8,2048]{2,1,0:T(8,128)(2,1)}), bf16[32,8,2048]{2,1,0:T(8,128)(2,1)S(1)}, u32[]{:S(2)}, u32[]{:S(2)}) %all-to-all-start.11) | async-done | bytes 1048608 | tf_op jit(solution)/shard_map/all_to_all | solution.py:62
  365.1 15.8 %all_to_all.82 = bf16[32,4,2048]{2,1,0:T(4,128)(2,1)S(1)} all-to-all(bf16[32,4,2048]{2,1,0:T(4,128)(2,1)S(1)} %bitcast.239), channel_id=1, replica_groups=mesh['segment'=16,'expert'=32] {'expert'}, dimensions={0} | all-to-all | bytes 1048576 | tf_op jit(solution)/shard_map/all_to_all | solution.py:110
  393.7 14.7 %all-to-all-done.14 = bf16[32,8,2048]{2,1,0:T(8,128)(2,1)S(1)} async-done(((bf16[32,8,2048]{2,1,0:T(8,128)(2,1)}), bf16[32,8,2048]{2,1,0:T(8,128)(2,1)S(1)}, u32[]{:S(2)}, u32[]{:S(2)}) %all-to-all-start.14) | async-done | bytes 1048608 | tf_op jit(solution)/shard_map/all_to_all | solution.py:22
  408.4 10.1 %all-to-all-start.13 = ((bf16[32,4,2048]{2,1,0:T(4,128)(2,1)}), bf16[32,4,2048]{2,1,0:T(4,128)(2,1)S(1)}, u32[]{:S(2)}, u32[]{:S(2)}) async-start(bf16[32,4,2048]{2,1,0:T(4,128)(2,1)} %reshape.250), calls=%async_computation.13 | async-start | bytes 1048576 | tf_op jit(solution)/shard_map/all_to_all | solution.py:115
  434.5 9.5 %all-to-all-start.15 = ((bf16[32,8,2048]{2,1,0:T(8,128)(2,1)}), bf16[32,8,2048]{2,1,0:T(8,128)(2,1)S(1)}, u32[]{:S(2)}, u32[]{:S(2)}) async-start(bf16[32,8,2048]{2,1,0:T(8,128)(2,1)} %fusion.3), calls=%async_computation.15 | async-start | bytes 2097152 | tf_op jit(solution)/shard_map/all_to_all | solution.py:62
  444.2 27.5 %all-to-all-done.15 = bf16[32,8,2048]{2,1,0:T(8,128)(2,1)S(1)} async-done(((bf16[32,8,2048]{2,1,0:T(8,128)(2,1)}), bf16[32,8,2048]{2,1,0:T(8,128)(2,1)S(1)}, u32[]{:S(2)}, u32[]{:S(2)}) %all-to-all-start.15) | async-done | bytes 1048608 | tf_op jit(solution)/shard_map/all_to_all | solution.py:62
  (168 shorter events, 122.3 us)
Async XLA Ops:
  0.0 49.1 %copy-start = (bf16[2,1,160,2048]{3,2,1,0:T(8,128)(2,1)S(1)}, bf16[2,1,160,2048]{3,2,1,0:T(8,128)(2,1)}, u32[]{:S(2)}) copy-start(bf16[2,1,160,2048]{3,2,1,0:T(8,128)(2,1)} %param.16) | copy-start | bytes 3932164
  2.3 34.1 %copy-start.20 = (s32[8,2]{0,1:T(2,128)}, s32[8,2]{0,1:T(2,128)S(1)}, u32[]{:S(2)}) copy-start(s32[8,2]{0,1:T(2,128)S(1)} %get-tuple-element.30) | copy-start | bytes 196
  3.8 32.6 %copy-start.3 = (f32[8,4]{0,1:T(4,128)}, f32[8,4]{0,1:T(4,128)S(1)}, u32[]{:S(2)}) copy-start(f32[8,4]{0,1:T(4,128)S(1)} %get-tuple-element.40) | copy-start | bytes 388
  7.3 28.0 %all-to-all-start = ((bf16[32,4,2048]{2,1,0:T(4,128)(2,1)}), bf16[32,4,2048]{2,1,0:T(4,128)(2,1)S(1)}, u32[]{:S(2)}, u32[]{:S(2)}) async-start(bf16[32,4,2048]{2,1,0:T(4,128)(2,1)} %bitcast.6), calls=%async_computation | async-start | bytes 1048576 | tf_op jit(solution)/shard_map/all_to_all | solution.py:110
  36.4 32.3 %all-to-all-start.2 = ((bf16[32,8,2048]{2,1,0:T(8,128)(2,1)}), bf16[32,8,2048]{2,1,0:T(8,128)(2,1)S(1)}, u32[]{:S(2)}, u32[]{:S(2)}) async-start(bf16[32,8,2048]{2,1,0:T(8,128)(2,1)} %broadcast_in_dim.169), calls=%async_computation.2 | async-start | bytes 2097152 | tf_op jit(solution)/shard_map/all_to_all | solution.py:22
  68.7 22.3 %all-to-all-start.1 = ((bf16[32,4,2048]{2,1,0:T(4,128)(2,1)}), bf16[32,4,2048]{2,1,0:T(4,128)(2,1)S(1)}, u32[]{:S(2)}, u32[]{:S(2)}) async-start(bf16[32,4,2048]{2,1,0:T(4,128)(2,1)} %reshape.232), calls=%async_computation.1 | async-start | bytes 1048576 | tf_op jit(solution)/shard_map/all_to_all | solution.py:115
  78.4 9.4 %collective-permute-start = (bf16[3,40,2048]{2,1,0:T(8,128)(2,1)S(1)}, bf16[3,40,2048]{2,1,0:T(8,128)(2,1)S(1)}, u32[]{:S(2)}, u32[]{:S(2)}) collective-permute-start(bf16[3,40,2048]{2,1,0:T(8,128)(2,1)S(1)} %pad_maximum_fusion), channel_id=1, source_target_pairs={{0,480},{32,0},{64,32},{96,64},{128,96},{160,128},{192,160},{224,1... | collective-permute-start | bytes 1474568 | tf_op jit(solution)/shard_map/ppermute | solution.py:34
  91.0 34.4 %all-to-all-start.3 = ((bf16[32,8,2048]{2,1,0:T(8,128)(2,1)}), bf16[32,8,2048]{2,1,0:T(8,128)(2,1)S(1)}, u32[]{:S(2)}, u32[]{:S(2)}) async-start(bf16[32,8,2048]{2,1,0:T(8,128)(2,1)} %fusion), calls=%async_computation.3 | async-start | bytes 2097152 | tf_op jit(solution)/shard_map/all_to_all | solution.py:62
  101.0 31.6 %copy-start.9 = (pred[8,4]{0,1:T(4,128)(4,1)}, pred[8,4]{0,1:T(4,128)(4,1)S(1)}, u32[]{:S(2)}) copy-start(pred[8,4]{0,1:T(4,128)(4,1)S(1)} %get-tuple-element.10) | copy-start | bytes 100
  125.8 6.6 %collective-permute-start.1 = (bf16[8,2048]{1,0:T(8,128)(2,1)S(1)}, bf16[8,2048]{1,0:T(8,128)(2,1)S(1)}, u32[]{:S(2)}, u32[]{:S(2)}) collective-permute-start(bf16[8,2048]{1,0:T(8,128)(2,1)S(1)} %fusion.8), channel_id=1, source_target_pairs={{0,32},{32,64},{64,96},{96,128},{128,160},{160,192},{192,224},{224... | collective-permute-start | bytes 98312 | tf_op jit(solution)/shard_map/ppermute | solution.py:34
  151.1 29.2 %all-to-all-start.6 = ((bf16[32,8,2048]{2,1,0:T(8,128)(2,1)}), bf16[32,8,2048]{2,1,0:T(8,128)(2,1)S(1)}, u32[]{:S(2)}, u32[]{:S(2)}) async-start(bf16[32,8,2048]{2,1,0:T(8,128)(2,1)} %broadcast_in_dim.175), calls=%async_computation.6 | async-start | bytes 2097152 | tf_op jit(solution)/shard_map/all_to_all | solution.py:22
  180.3 26.9 %all-to-all-start.5 = ((bf16[32,4,2048]{2,1,0:T(4,128)(2,1)}), bf16[32,4,2048]{2,1,0:T(4,128)(2,1)S(1)}, u32[]{:S(2)}, u32[]{:S(2)}) async-start(bf16[32,4,2048]{2,1,0:T(4,128)(2,1)} %reshape.238), calls=%async_computation.5 | async-start | bytes 1048576 | tf_op jit(solution)/shard_map/all_to_all | solution.py:115
  190.6 13.8 %collective-permute-start.2 = (bf16[3,40,2048]{2,1,0:T(8,128)(2,1)S(1)}, bf16[3,40,2048]{2,1,0:T(8,128)(2,1)S(1)}, u32[]{:S(2)}, u32[]{:S(2)}) collective-permute-start(bf16[3,40,2048]{2,1,0:T(8,128)(2,1)S(1)} %pad_maximum_fusion.1), channel_id=1, source_target_pairs={{0,480},{32,0},{64,32},{96,64},{128,96},{160,128},{192,160},{224,1... | collective-permute-start | bytes 1474568 | tf_op jit(solution)/shard_map/ppermute | solution.py:34
  207.2 36.1 %all-to-all-start.7 = ((bf16[32,8,2048]{2,1,0:T(8,128)(2,1)}), bf16[32,8,2048]{2,1,0:T(8,128)(2,1)S(1)}, u32[]{:S(2)}, u32[]{:S(2)}) async-start(bf16[32,8,2048]{2,1,0:T(8,128)(2,1)} %fusion.1), calls=%async_computation.7 | async-start | bytes 2097152 | tf_op jit(solution)/shard_map/all_to_all | solution.py:62
  244.3 4.4 collective-permute-start.3
  272.3 31.5 %all-to-all-start.10 = ((bf16[32,8,2048]{2,1,0:T(8,128)(2,1)}), bf16[32,8,2048]{2,1,0:T(8,128)(2,1)S(1)}, u32[]{:S(2)}, u32[]{:S(2)}) async-start(bf16[32,8,2048]{2,1,0:T(8,128)(2,1)} %broadcast_in_dim.181), calls=%async_computation.10 | async-start | bytes 2097152 | tf_op jit(solution)/shard_map/all_to_all | solution.py:22
  303.8 21.9 %all-to-all-start.9 = ((bf16[32,4,2048]{2,1,0:T(4,128)(2,1)}), bf16[32,4,2048]{2,1,0:T(4,128)(2,1)S(1)}, u32[]{:S(2)}, u32[]{:S(2)}) async-start(bf16[32,4,2048]{2,1,0:T(4,128)(2,1)} %reshape.244), calls=%async_computation.9 | async-start | bytes 1048576 | tf_op jit(solution)/shard_map/all_to_all | solution.py:115
  312.9 8.6 %collective-permute-start.4 = (bf16[3,40,2048]{2,1,0:T(8,128)(2,1)S(1)}, bf16[3,40,2048]{2,1,0:T(8,128)(2,1)S(1)}, u32[]{:S(2)}, u32[]{:S(2)}) collective-permute-start(bf16[3,40,2048]{2,1,0:T(8,128)(2,1)S(1)} %pad_maximum_fusion.2), channel_id=1, source_target_pairs={{0,480},{32,0},{64,32},{96,64},{128,96},{160,128},{192,160},{224,1... | collective-permute-start | bytes 1474568 | tf_op jit(solution)/shard_map/ppermute | solution.py:34
  325.8 32.4 %all-to-all-start.11 = ((bf16[32,8,2048]{2,1,0:T(8,128)(2,1)}), bf16[32,8,2048]{2,1,0:T(8,128)(2,1)S(1)}, u32[]{:S(2)}, u32[]{:S(2)}) async-start(bf16[32,8,2048]{2,1,0:T(8,128)(2,1)} %fusion.2), calls=%async_computation.11 | async-start | bytes 2097152 | tf_op jit(solution)/shard_map/all_to_all | solution.py:62
  358.6 5.8 %collective-permute-start.5 = (bf16[8,2048]{1,0:T(8,128)(2,1)S(1)}, bf16[8,2048]{1,0:T(8,128)(2,1)S(1)}, u32[]{:S(2)}, u32[]{:S(2)}) collective-permute-start(bf16[8,2048]{1,0:T(8,128)(2,1)S(1)} %fusion.10), channel_id=1, source_target_pairs={{0,32},{32,64},{64,96},{96,128},{128,160},{160,192},{192,224},{224... | collective-permute-start | bytes 98312 | tf_op jit(solution)/shard_map/ppermute | solution.py:34
  382.0 26.4 %all-to-all-start.14 = ((bf16[32,8,2048]{2,1,0:T(8,128)(2,1)}), bf16[32,8,2048]{2,1,0:T(8,128)(2,1)S(1)}, u32[]{:S(2)}, u32[]{:S(2)}) async-start(bf16[32,8,2048]{2,1,0:T(8,128)(2,1)} %broadcast_in_dim.187), calls=%async_computation.14 | async-start | bytes 2097152 | tf_op jit(solution)/shard_map/all_to_all | solution.py:22
  408.4 26.1 %all-to-all-start.13 = ((bf16[32,4,2048]{2,1,0:T(4,128)(2,1)}), bf16[32,4,2048]{2,1,0:T(4,128)(2,1)S(1)}, u32[]{:S(2)}, u32[]{:S(2)}) async-start(bf16[32,4,2048]{2,1,0:T(4,128)(2,1)} %reshape.250), calls=%async_computation.13 | async-start | bytes 1048576 | tf_op jit(solution)/shard_map/all_to_all | solution.py:115
  419.6 12.1 %collective-permute-start.6 = (bf16[3,40,2048]{2,1,0:T(8,128)(2,1)S(1)}, bf16[3,40,2048]{2,1,0:T(8,128)(2,1)S(1)}, u32[]{:S(2)}, u32[]{:S(2)}) collective-permute-start(bf16[3,40,2048]{2,1,0:T(8,128)(2,1)S(1)} %pad_maximum_fusion.3), channel_id=1, source_target_pairs={{0,480},{32,0},{64,32},{96,64},{128,96},{160,128},{192,160},{224,1... | collective-permute-start | bytes 1474568 | tf_op jit(solution)/shard_map/ppermute | solution.py:34
  434.5 37.1 %all-to-all-start.15 = ((bf16[32,8,2048]{2,1,0:T(8,128)(2,1)}), bf16[32,8,2048]{2,1,0:T(8,128)(2,1)S(1)}, u32[]{:S(2)}, u32[]{:S(2)}) async-start(bf16[32,8,2048]{2,1,0:T(8,128)(2,1)} %fusion.3), calls=%async_computation.15 | async-start | bytes 2097152 | tf_op jit(solution)/shard_map/all_to_all | solution.py:62
  (21 other events, 307.0 us)
where the time goes:
time: 475 us; the launch traced here: 473 us
  waiting for transfers between devices  223 us (47%)
  starting transfers between devices  138 us (29%)
  blocking collectives  54.7 us (12%)
  matrix products  28.6 us (6%)
  local copies, waits for them, and re-layouts  18.4 us (4%)
  other arithmetic  10 us (2%)
    all_to_all x4, waiting for transfers between devices, spare_served(): lax.all_to_all(gathered.reshape(members, tok_dev, model_width), 'expert',...  101 us
    all_to_all x4, waiting for transfers between devices, sent_to_all(): lax.all_to_all(jnp.broadcast_to(shard[None], (peers, *shard.shape)), axis...  69.4 us
    all_to_all x3, blocking collectives, on_device(): lax.all_to_all(outgoing, 'expert', split_axis=0, concat_axis=0, tiled=True)  54.7 us
    ppermute x7, waiting for transfers between devices, from_behind(): return lax.ppermute(value, axis, pairs)  36.2 us
    all_to_all x4, starting transfers between devices, spare_served(): lax.all_to_all(gathered.reshape(members, tok_dev, model_width), 'expert',...  35.7 us
    all_to_all x4, starting transfers between devices, on_device(): lax.all_to_all(partial_value.reshape(members, slot_count, model_width), '...  35.7 us
    all_to_all x4, starting transfers between devices, sent_to_all(): lax.all_to_all(jnp.broadcast_to(shard[None], (peers, *shard.shape)), axis...  28.1 us
    ppermute x7, starting transfers between devices, from_behind(): return lax.ppermute(value, axis, pairs)  24.5 us
  transfers between devices with their start and end apart: 20, of which 18 were waited for; matrix products, arithmetic and copies ran while one was open for 9% of the time, Pallas kernels for 0%

commit v1 on v0

v1 whole, which is shorter than its diff:
```python
import functools

import jax
import jax.numpy as jnp
from jax import lax
from jax.experimental import pallas as pl
from jax.experimental.pallas import tpu as pltpu
from jax.sharding import PartitionSpec as P

EXPERTS = 4
TICKS = 4
CAP = 4
EPSILON = 1e-06
LANES = 128
MESH = pl.DeviceIdType.MESH
F32 = jnp.float32
BF16 = jnp.bfloat16

BZ_NEAR, BZ_FAR, BX_WHOLE, BX_HALF, AX, AZ = 0, 4, 7, 9, 11, 14
RBX_HALF, RBX_WHOLE, RAZ, RBZ, RAX = 22, 24, 26, 34, 41
COPIES = 44


def group_of(section, tick_idx, segments):
    start = lax.rem(section - tick_idx + segments, segments)
    odd = lax.rem(start, 2) == 1
    first = jnp.where(odd & (start + TICKS <= segments), 1, 0)
    return first + jnp.where(start + tick_idx >= segments, 1, 0)


def kernel(
    segments, nx, nz,
    state, routes, gates, gain, w_gate, w_up, w_down, spare_g, spare_u, spare_d,
    out,
    cur, nxt, coef, gw, uw, dw, xa, xb, pa, pb, ra1, ra, qf, qa, rqa, rb1, rb2, sb, rz,
    send_sem, recv_sem, shift_send, shift_recv, w_sem, spare_send, spare_recv,
):
    tok, width = state.shape
    aw = pa.shape[-1]
    bw = pb.shape[-1]
    rows = nx * nz * tok
    home, extra = w_gate.shape[1], spare_g.shape[1]
    slices = gw.shape[1]
    s = lax.axis_index("segment")
    mine = lax.axis_index("expert")
    x, z = mine // nz, lax.rem(mine, nz)
    half_z, half_x = nz // 2, nx // 2
    odd = lax.rem(z, 2)
    turn = 1 - 2 * odd

    def xo(k):
        return lax.rem(x + k + nx, nx)

    def zo(k):
        return lax.rem(z + k + nz, nz)

    def at(xx, zz):
        return (s, xx * nz + zz)

    after = (lax.rem(s + 1, segments), mine)
    before = (lax.rem(s + segments - 1, segments), mine)

    loads = []
    for i, (source, store) in enumerate(((w_gate, gw), (w_up, uw), (w_down, dw))):
        load = pltpu.make_async_copy(source, store.at[:, pl.ds(0, home)], w_sem.at[i])
        load.start()
        loads.append(load)

    barrier = pltpu.get_barrier_semaphore()
    peers = [at(xo(1), z), at(xo(2), z), at(xo(3), z)]
    peers += [at(x, zo(1)), at(x, zo(-1)), at(x, zo(2)), at(x, zo(-2)), after, before]
    for peer in peers:
        pl.semaphore_signal(barrier, inc=1, device_id=peer, device_id_type=MESH)

    for store in (gw, uw, dw):
        store[:, home + extra :] = jnp.zeros((2, slices - home - extra, tok, width), BF16)
    cur[0] = state[...]

    lane = lax.broadcasted_iota(jnp.int32, (tok, LANES), 1)
    row = lax.broadcasted_iota(jnp.int32, (tok, LANES), 0)
    label, low, of_tick = lane % 8, (lane // 8) % 2, lane // 16
    packed = jnp.zeros((tok, LANES), F32)
    for t in range(TICKS):
        chosen, weights = routes[t], gates[t]
        hit0, hit1 = chosen[:, 0:1] == label, chosen[:, 1:2] == label
        member = jnp.where(hit0 | hit1, 1.0, 0.0)
        whole = jnp.where(hit0, weights[:, 0:1], 0.0) + jnp.where(hit1, weights[:, 1:2], 0.0)
        position = jnp.zeros((tok, LANES), F32)
        for i in range(tok - 1):
            position = position + jnp.where(row > i, member[i : i + 1], 0.0)
        inside = position < CAP
        over = jnp.where(inside | (lane >= EXPERTS), 0.0, whole)
        spill = jnp.sum(over, axis=1, keepdims=True)
        value = jnp.where(label == EXPERTS, spill, jnp.where(inside, whole, 0.0))
        top = value.astype(BF16).astype(F32)
        packed = jnp.where(of_tick == t, jnp.where(low == 1, value - top, top), packed)
    coef[...] = packed.astype(BF16)

    pl.semaphore_wait(barrier, len(peers))

    first_there = group_of(before[0], 0, segments)
    first_here = group_of(s, 0, segments)
    spares = []
    for order in range(2):
        there = first_there if order == 0 else 1 - first_there
        for i, (source, store) in enumerate(((spare_g, gw), (spare_u, uw), (spare_d, dw))):
            copy = pltpu.make_async_remote_copy(
                source.at[there],
                store.at[there, pl.ds(home, extra)],
                spare_send.at[order, i],
                spare_recv.at[order, i],
                device_id=before,
                device_id_type=MESH,
            )
            copy.start()
            spares.append(copy)

    def spare_wait(order):
        here = first_here if order == 0 else 1 - first_here
        for i, (source, store) in enumerate(((spare_g, gw), (spare_u, uw), (spare_d, dw))):
            pltpu.make_async_remote_copy(
                source.at[here],
                store.at[here, pl.ds(home, extra)],
                spare_send.at[order, i],
                spare_recv.at[order, i],
                device_id=before,
                device_id_type=MESH,
            ).wait_recv()

    def shift_copy(t):
        return pltpu.make_async_remote_copy(
            nxt.at[t],
            cur.at[t + 1],
            shift_send.at[t],
            shift_recv.at[t],
            device_id=after,
            device_id_type=MESH,
        )

    def tick(t, carry):
        group = group_of(s, t, segments)
        started = []

        def send(number, source, target, peer):
            copy = pltpu.make_async_remote_copy(
                source,
                target,
                send_sem.at[t, number],
                recv_sem.at[t, number],
                device_id=peer,
                device_id_type=MESH,
            )
            copy.start()
            started.append(copy)

        def arrived(number, landing):
            pltpu.make_async_remote_copy(
                landing,
                landing,
                send_sem.at[t, number],
                recv_sem.at[t, number],
                device_id=after,
                device_id_type=MESH,
            ).wait_recv()

        @pl.when(t > 0)
        def _():
            shift_copy(t - 1).wait_recv()

        values = cur[t].astype(F32)
        scale = lax.rsqrt(jnp.mean(values * values, axis=-1, keepdims=True) + EPSILON)
        normed = (values * scale * gain[group]).astype(BF16)
        xa[t, z, x, :, :aw] = normed[:, :aw]
        xa[t, z, x, :, aw:] = coef[...]
        xb[t, z, x] = normed[:, aw:]

        for off in (1, 2, 3):
            send(AX + off - 1, xa.at[t, z, x], xa.at[t, z, x], at(xo(off), z))
        for i, off in enumerate((1, -1, 2, -2)):
            send(BZ_NEAR + i, xb.at[t, z, x], xb.at[t, z, x], at(x, zo(off)))

        def a_step(k):
            if k == 4:
                right, left = pl.ds(0, half_x), pl.ds(half_x, half_x)
            else:
                right = left = pl.ds(0, nx)
            block = xa.at[t, zo(1 - k), right]
            send(AZ + 2 * k - 2, block, block, at(x, zo(1)))
            block = xa.at[t, zo(k - 1), left]
            send(AZ + 2 * k - 1, block, block, at(x, zo(-1)))

        def a_arrived(k):
            if k == 4:
                right, left = pl.ds(0, half_x), pl.ds(half_x, half_x)
            else:
                right = left = pl.ds(0, nx)
            arrived(AZ + 2 * k - 2, xa.at[t, zo(-k), right])
            arrived(AZ + 2 * k - 1, xa.at[t, zo(k), left])

        for i, off in enumerate((1, -1, 2, -2)):
            arrived(BZ_NEAR + i, xb.at[t, zo(-off), x])
        block = xb.at[t, zo(-2), x]
        send(BZ_FAR, block, block, at(x, zo(1)))
        block = xb.at[t, zo(2), x]
        send(BZ_FAR + 1, block, block, at(x, zo(-1)))
        block = xb.at[t, zo(-2 * turn), x]
        send(BZ_FAR + 2, block, block, at(x, zo(2 * turn)))
        for off in (1, 2, 3):
            arrived(AX + off - 1, xa.at[t, z, xo(-off)])
        a_step(1)
        arrived(BZ_FAR, xb.at[t, zo(-3), x])
        arrived(BZ_FAR + 1, xb.at[t, zo(3), x])
        arrived(BZ_FAR + 2, xb.at[t, zo(4), x])
        block = xb.at[t, :, x]
        send(BX_WHOLE, block, block, at(xo(1), z))
        send(BX_WHOLE + 1, block, block, at(xo(-1), z))
        a_arrived(1)
        a_step(2)
        a_arrived(2)
        a_step(3)
        arrived(BX_WHOLE, xb.at[t, :, xo(-1)])
        block = xb.at[t, pl.ds(0, half_z), xo(-1)]
        send(BX_HALF, block, block, at(xo(1), z))
        arrived(BX_WHOLE + 1, xb.at[t, :, xo(1)])
        block = xb.at[t, pl.ds(half_z, half_z), xo(1)]
        send(BX_HALF + 1, block, block, at(xo(-1), z))
        a_arrived(3)
        a_step(4)

        @pl.when(t == 0)
        def _():
            for load in loads:
                load.wait()
            spare_wait(0)

        @pl.when(t == 1)
        def _():
            spare_wait(1)

        arrived(BX_HALF, xb.at[t, pl.ds(0, half_z), xo(2)])
        arrived(BX_HALF + 1, xb.at[t, pl.ds(half_z, half_z), xo(2)])
        a_arrived(4)

        a_rows = xa.at[t].reshape(rows, aw + LANES)
        b_rows = xb.at[t].reshape(rows, bw)
        gate_w = gw.at[group].reshape(slices * tok, width)
        up_w = uw.at[group].reshape(slices * tok, width)
        down_w = dw.at[group].reshape(slices * tok, width)
        contract = (((1,), (1,)), ((), ()))

        def product(weight):
            return lax.dot_general(
                a_rows[:, :aw], weight[:, :aw], contract, preferred_element_type=F32
            ) + lax.dot_general(b_rows[...], weight[:, aw:], contract, preferred_element_type=F32)

        gate = product(gate_w)
        up = product(up_w)
        factors = a_rows[:, aw:].astype(F32)
        lanes = lax.broadcasted_iota(jnp.int32, factors.shape, 1)
        base = t * 16

        def factor(which):
            spot = (lanes == base + which) | (lanes == base + which + 8)
            return jnp.sum(jnp.where(spot, factors, 0.0), axis=1, keepdims=True)

        units = lax.broadcasted_iota(jnp.int32, gate.shape, 1)
        scales = jnp.where(units < home * tok, factor(x), factor(EXPERTS))
        hidden = (gate / (1.0 + jnp.exp(-gate)) * up * scales).astype(BF16)
        pb.reshape(rows, bw)[...] = jnp.dot(
            hidden, down_w[:, aw:], preferred_element_type=F32
        ).astype(BF16)

        send(RBX_HALF, pb.at[pl.ds(0, half_z), xo(2)], rb1.at[t, 0], at(xo(1), z))
        send(RBX_HALF + 1, pb.at[pl.ds(half_z, half_z), xo(2)], rb1.at[t, 1], at(xo(-1), z))
        pa.reshape(rows, aw)[...] = jnp.dot(
            hidden, down_w[:, :aw], preferred_element_type=F32
        ).astype(BF16)
        send(RAZ, pa.at[zo(4), pl.ds(0, half_x)], ra1.at[t, 0], at(x, zo(1)))
        send(RAZ + 1, pa.at[zo(4), pl.ds(half_x, half_x)], ra1.at[t, 1], at(x, zo(-1)))

        def plus(first, *more):
            total = first.astype(F32)
            for term in more:
                total = total + term.astype(F32)
            return total

        def add_first(side):
            cut = pl.ds(side * half_x, half_x)
            to = zo(3 - 6 * side)
            arrived(RAZ + side, ra1.at[t, side])
            pa[to, cut] = plus(pa[to, cut], ra1[t, side]).astype(BF16)
            send(RAZ + 2 + side, pa.at[to], ra.at[t, 0, side], at(x, zo(1 - 2 * side)))

        def add_next(side, k):
            to = zo((4 - k) * (1 - 2 * side))
            arrived(RAZ + 2 * k - 2 + side, ra.at[t, k - 2, side])
            pa[to] = plus(pa[to], ra[t, k - 2, side]).astype(BF16)
            send(RAZ + 2 * k + side, pa.at[to], ra.at[t, k - 1, side], at(x, zo(1 - 2 * side)))

        def add_b(side):
            cut = pl.ds(side * half_z, half_z)
            to = xo(1 - 2 * side)
            arrived(RBX_HALF + side, rb1.at[t, side])
            pb[cut, to] = plus(pb[cut, to], rb1[t, side]).astype(BF16)
            send(RBX_WHOLE + side, pb.at[:, to], rb2.at[t, side], at(to, z))

        add_b(0)
        add_b(1)
        add_first(0)
        add_first(1)
        for k in (2, 3):
            add_next(0, k)
            add_next(1, k)
        arrived(RBX_WHOLE, rb2.at[t, 0])
        arrived(RBX_WHOLE + 1, rb2.at[t, 1])
        sb[...] = plus(pb[:, x], rb2[t, 0], rb2[t, 1]).astype(BF16)
        send(RBZ + 4, sb.at[zo(4)], rz.at[t, 4], at(x, zo(2 * turn)))
        send(RBZ + 2, sb.at[zo(3)], rz.at[t, 2], at(x, zo(1)))
        send(RBZ + 3, sb.at[zo(-3)], rz.at[t, 3], at(x, zo(-1)))
        send(RBZ, sb.at[zo(1)], rz.at[t, 0], at(x, zo(1)))
        send(RBZ + 1, sb.at[zo(-1)], rz.at[t, 1], at(x, zo(-1)))
        arrived(RAZ + 6, ra.at[t, 2, 0])
        arrived(RAZ + 7, ra.at[t, 2, 1])
        total = plus(pa[z], ra[t, 2, 0], ra[t, 2, 1])
        qf[...] = total
        qa[...] = total.astype(BF16)
        for off in (1, 2, 3):
            send(RAX + off - 1, qa.at[xo(off)], rqa.at[t, off - 1], at(xo(off), z))
        for i in (2, 3, 4):
            arrived(RBZ + i, rz.at[t, i])
        far, near = zo(2 * turn), zo(-2 * turn)
        sb[far] = plus(sb[far], rz[t, 2 + odd], rz[t, 4]).astype(BF16)
        sb[near] = plus(sb[near], rz[t, 3 - odd]).astype(BF16)
        send(RBZ + 5, sb.at[zo(2)], rz.at[t, 5], at(x, zo(2)))
        send(RBZ + 6, sb.at[zo(-2)], rz.at[t, 6], at(x, zo(-2)))
        for i in (0, 1):
            arrived(RBZ + i, rz.at[t, i])
        part_b = plus(pb[z, x], rb2[t, 0, z], rb2[t, 1, z], rz[t, 0], rz[t, 1])
        for off in (1, 2, 3):
            arrived(RAX + off - 1, rqa.at[t, off - 1])
        part_a = plus(qf[x], rqa[t, 0], rqa[t, 1], rqa[t, 2])
        nxt[t, :, :aw] = (cur[t, :, :aw].astype(F32) + part_a).astype(BF16)
        for i in (5, 6):
            arrived(RBZ + i, rz.at[t, i])
        part_b = plus(part_b, rz[t, 5], rz[t, 6])
        nxt[t, :, aw:] = (cur[t, :, aw:].astype(F32) + part_b).astype(BF16)

        @pl.when(t + 1 < TICKS)
        def _():
            shift_copy(t).start()

        for copy in started:
            copy.wait_send()
        return carry

    lax.fori_loop(0, TICKS, tick, 0)
    out[...] = nxt[TICKS - 1]
    for t in range(TICKS - 1):
        shift_copy(t).wait_send()
    for copy in spares:
        copy.wait_send()


def on_device(
    state, routes, gates, norm_gain, w_gate, w_up, w_down, spare_gate, spare_up, spare_down
):
    segments = lax.axis_size("segment")
    members = lax.axis_size("expert")
    nx = EXPERTS
    nz = members // nx
    tok, width = state.shape[1:]
    aw = max(1, width // LANES * 7 // 16) * LANES
    bw = width - aw
    home, extra = w_gate.shape[2], spare_gate.shape[2]
    units = -(-(home + extra) // 256) * 256

    def cut(weights):
        return weights.reshape(2, weights.shape[2] // tok, tok, width)

    vmem, anywhere = pl.BlockSpec(memory_space=pltpu.VMEM), pl.BlockSpec(memory_space=pl.ANY)
    store = pltpu.VMEM((2, units // tok, tok, width), BF16)
    final = pl.pallas_call(
        functools.partial(kernel, segments, nx, nz),
        out_shape=jax.ShapeDtypeStruct((tok, width), BF16),
        in_specs=[vmem] * 4 + [anywhere] * 6,
        out_specs=vmem,
        scratch_shapes=[
            pltpu.VMEM((TICKS, tok, width), BF16),
            pltpu.VMEM((TICKS, tok, width), BF16),
            pltpu.VMEM((tok, LANES), BF16),
            store,
            store,
            store,
            pltpu.VMEM((TICKS, nz, nx, tok, aw + LANES), BF16),
            pltpu.VMEM((TICKS, nz, nx, tok, bw), BF16),
            pltpu.VMEM((nz, nx, tok, aw), BF16),
            pltpu.VMEM((nz, nx, tok, bw), BF16),
            pltpu.VMEM((TICKS, 2, nx // 2, tok, aw), BF16),
            pltpu.VMEM((TICKS, 3, 2, nx, tok, aw), BF16),
            pltpu.VMEM((nx, tok, aw), F32),
            pltpu.VMEM((nx, tok, aw), BF16),
            pltpu.VMEM((TICKS, 3, tok, aw), BF16),
            pltpu.VMEM((TICKS, 2, nz // 2, tok, bw), BF16),
            pltpu.VMEM((TICKS, 2, nz, tok, bw), BF16),
            pltpu.VMEM((nz, tok, bw), BF16),
            pltpu.VMEM((TICKS, 7, tok, bw), BF16),
            pltpu.SemaphoreType.DMA((TICKS, COPIES)),
            pltpu.SemaphoreType.DMA((TICKS, COPIES)),
            pltpu.SemaphoreType.DMA((TICKS - 1,)),
            pltpu.SemaphoreType.DMA((TICKS - 1,)),
            pltpu.SemaphoreType.DMA((3,)),
            pltpu.SemaphoreType.DMA((2, 3)),
            pltpu.SemaphoreType.DMA((2, 3)),
        ],
        compiler_params=pltpu.CompilerParams(
            collective_id=0, has_side_effects=True, vmem_limit_bytes=44 * 1024 * 1024
        ),
    )(
        state[0],
        routes[:, 0],
        gates[:, 0],
        norm_gain,
        cut(w_gate),
        cut(w_up),
        cut(w_down),
        cut(spare_gate),
        cut(spare_up),
        cut(spare_down),
    )
    return final[None]


def solution(mesh):
    return jax.shard_map(
        on_device,
        mesh=mesh,
        in_specs=(
            P("segment", "expert", None),
            P(None, "segment", "expert", None),
            P(None, "segment", "expert", None),
            P(None, "segment", None),
            P(None, "segment", "expert", None),
            P(None, "segment", "expert", None),
            P(None, "segment", "expert", None),
            P(None, "segment", "expert", None),
            P(None, "segment", "expert", None),
            P(None, "segment", "expert", None),
        ),
        out_specs=P("segment", "expert", None),
        check_vma=False,
    )
```

time: 475 us -> 193 us (0.41)
  the two profiles are of different devices: /device:TPU:1 before, /device:TPU:16 now
where the time goes in v1:
time: 193 us; the launch traced here: 192 us
  Pallas kernels  182 us (94%)
  local copies, waits for them, and re-layouts  10.5 us (5%)
    pallas_call x1, Pallas kernels, on_device(): pl.pallas_call(functools.partial(kernel, segments, nx, nz), out_shape=jax...  182 us
    unnamed x17, local copies, waits for them, and re-layouts  8.96 us

profile of v1, /device:TPU:16, one launch (start us, length us, event | category | flops | bytes accessed | tf_op | source)
XLA Modules:
  0.0 192.1 jit_solution(2223790226068706021)
XLA Ops:
  0.0 0.8 copy.13.routes
  0.8 0.8 copy.14.gates
  1.6 0.0 copy-start
  1.6 1.3 copy-done
  2.9 0.0 copy-start.1
  2.9 1.3 copy-done.1
  4.2 0.0 copy-start.2
  4.2 1.3 copy-done.2
  5.5 0.0 copy-start.3
  5.5 1.0 copy-done.3
  6.5 0.0 copy-start.4
  6.5 1.0 copy-done.4
  7.5 0.0 copy-start.5
  7.5 1.0 copy-done.5
  8.4 0.0 copy-start.6
  8.4 0.8 copy-done.6
  9.2 0.0 copy-start.7
  9.2 0.7 copy-done.7
  9.9 181.6 %shard_map.100 = bf16[8,2048]{1,0:T(8,128)(2,1)S(1)} custom-call(bf16[8,2048]{1,0:T(8,128)(2,1)S(1)} %bitcast.17, s32[4,8,2]{2,1,0:T(8,128)S(1)} %copy.13.routes, f32[4,8,2]{2,1,0:T(8,128)S(1)} %copy.14.gates, f32[2,1,2048]{2,1,0:T(1,128)S(1)} %copy-done.7, bf16[2,20,8,2048]{3,2,1,0:T(8,128)(2,1)S(1)} %bitcast.10, bf16[2,20,8,2048]{3,2,1,0:T(8,128)(2,1)S(1)} %bitcast.11, ...), custom_call_target="tpu_custom_call" | custom-call | tf_op jit(solution)/shard_map/pallas_call | solution.py:382
  191.5 0.6 copy.20
Async XLA Ops:
  1.6 1.3 copy-start
  2.9 1.3 copy-start.1
  4.2 1.3 copy-start.2
  5.5 1.0 copy-start.3
  6.5 1.0 copy-start.4
  7.5 1.0 copy-start.5
  8.4 0.8 copy-start.6
  9.2 0.7 copy-start.7

commit v2 on v0

v2 whole, which is shorter than its diff:
```python
import functools
import math

import jax
import jax.numpy as jnp
from jax import lax
from jax.experimental import pallas as pl
from jax.experimental.pallas import tpu as pltpu
from jax.sharding import PartitionSpec as P

EXPERTS = 4
TICKS = 4
CAP = 4
EPSILON = 1e-06
LANES = 128
MESH = pl.DeviceIdType.MESH
F32 = jnp.float32
BF16 = jnp.bfloat16

def group_of(section, tick_idx, segments):
    start = lax.rem(section - tick_idx + segments, segments)
    odd = lax.rem(start, 2) == 1
    first = jnp.where(odd & (start + TICKS <= segments), 1, 0)
    return first + jnp.where(start + tick_idx >= segments, 1, 0)


ORDER = (0, 1, -1, 2, -2, 3, -3, 4)
NZ, NX = 8, 4
GZ, GX, SX, SZ = 0, 8, 32, 56
COPIES = 64


def slot_from(offset):
    return next(i for i, d in enumerate(ORDER) if (d + offset) % NZ == 0)


def flat(ref):
    return ref.reshape(math.prod(ref.shape[:-1]), ref.shape[-1])


def put(ref, value):
    flat(ref)[...] = value


def kernel(
    segments,
    state, routes, gates, gain, w_gate, w_up, w_down, spare_g, spare_u, spare_d,
    out,
    cur, routes_v, gates_v, gain_v, coef, gw, uw, dw, xb, hid, pb, rx, sb, res, parts,
    send_sem, recv_sem, res_send, res_recv, w_sem, spare_send, spare_recv, coef_send, coef_recv,
):
    tok, width = state.shape
    home, extra = w_gate.shape[1], spare_g.shape[1]
    units = gw.shape[1] * tok
    half = NZ // 2
    rows = half * NX * tok
    s = lax.axis_index("segment")
    mine = lax.axis_index("expert")
    x, z = mine // NZ, lax.rem(mine, NZ)
    s_after = lax.rem(s + 1, segments)
    s_before = lax.rem(s + segments - 1, segments)

    def at(section, off_x, off_z):
        return (section, lax.rem(x + off_x + NX, NX) * NZ + lax.rem(z + off_z + NZ, NZ))

    before, after = (s_before, mine), (s_after, mine)

    loads = []
    for i, (source, store) in enumerate(
        (
            (state, cur.at[0]),
            (routes, routes_v),
            (gates, gates_v),
            (gain, gain_v),
            (w_gate, gw.at[:, pl.ds(0, home)]),
            (w_up, uw.at[:, pl.ds(0, home)]),
            (w_down, dw.at[:, pl.ds(0, home)]),
        )
    ):
        load = pltpu.make_async_copy(source, store, w_sem.at[i])
        load.start()
        loads.append(load)

    barrier = pltpu.get_barrier_semaphore()
    peers = [at(s, off, 0) for off in range(1, NX)]
    peers += [at(s, 0, off) for off in range(1, NZ)]
    for section in (s_after, s_before):
        peers += [at(section, 0, off) for off in range(NZ)]
    for peer in peers:
        pl.semaphore_signal(barrier, inc=1, device_id=peer, device_id_type=MESH)

    for store in (gw, uw, dw):
        unused = gw.shape[1] - home - extra
        store[:, home + extra :] = jnp.zeros((2, unused, tok, width), BF16)

    lane = lax.broadcasted_iota(jnp.int32, (tok, LANES), 1)
    row = lax.broadcasted_iota(jnp.int32, (tok, LANES), 0)
    diagonal = row[:, :tok] == lane[:, :tok]
    label = (lane % 8).astype(F32)
    low, of_tick = (lane // 8) % 2, lane // 16

    def upright(line):
        line = jnp.broadcast_to(line, (tok, tok))
        return jnp.sum(jnp.where(diagonal, line, 0.0), axis=1, keepdims=True)

    for load in loads[:4]:
        load.wait()
    packed = jnp.zeros((tok, LANES), F32)
    for t in range(TICKS):
        chosen, weights = routes_v[t].astype(F32), gates_v[t]
        hit0, hit1 = upright(chosen[0:1]) == label, upright(chosen[1:2]) == label
        member = jnp.where(hit0 | hit1, 1.0, 0.0)
        whole = jnp.where(hit0, upright(weights[0:1]), 0.0)
        whole = whole + jnp.where(hit1, upright(weights[1:2]), 0.0)
        position = jnp.zeros((tok, LANES), F32)
        for i in range(tok - 1):
            position = position + jnp.where(row > i, member[i : i + 1], 0.0)
        inside = position < CAP
        over = jnp.where(inside | (lane >= EXPERTS), 0.0, whole)
        spill = jnp.sum(over, axis=1, keepdims=True)
        value = jnp.where(label == EXPERTS, spill, jnp.where(inside, whole, 0.0))
        top = value.astype(BF16).astype(F32)
        packed = jnp.where(of_tick == t, jnp.where(low == 1, value - top, top), packed)
    coef[0, 0] = packed.astype(BF16)

    pl.semaphore_wait(barrier, len(peers))

    def remote(source, target, sent, got, peer):
        return pltpu.make_async_remote_copy(
            source, target, sent, got, device_id=peer, device_id_type=MESH
        )

    first_there = group_of(s_before, 0, segments)
    first_here = group_of(s, 0, segments)
    spare_pairs = ((spare_g, gw), (spare_u, uw), (spare_d, dw))

    def spare_copy(order, i, first):
        source, store = spare_pairs[i]
        part = first if order == 0 else 1 - first
        return remote(
            source.at[part],
            store.at[part, pl.ds(home, extra)],
            spare_send.at[order, i],
            spare_recv.at[order, i],
            before,
        )

    def coef_z(j, peer):
        return remote(coef.at[0, 0], coef.at[j, 0], coef_send.at[j], coef_recv.at[j], peer)

    def coef_x(o, peer):
        n = NZ - 1 + o
        return remote(coef.at[:, 0], coef.at[:, o], coef_send.at[n], coef_recv.at[n], peer)

    def res_copy(t):
        return remote(cur.at[t], res.at[t], res_send.at[t], res_recv.at[t], after)

    def back_copy(t, i, peer):
        j = slot_from(ORDER[i])
        n = SZ + j
        return remote(sb.at[t, i], parts.at[t, j], send_sem.at[t, n], recv_sem.at[t, n], peer)

    def landed(t):
        for j in range(NZ - 1, -1, -1):
            target = parts.at[t, j]
            n = SZ + j
            if j == 0:
                @pl.when(t < TICKS - 1)
                def _():
                    remote(target, target, send_sem.at[t, n], recv_sem.at[t, n], after).wait_recv()
            else:
                remote(target, target, send_sem.at[t, n], recv_sem.at[t, n], after).wait_recv()
        total = parts[t, NZ - 1].astype(F32)
        for j in range(NZ - 2, -1, -1):
            total = total + parts[t, j].astype(F32)
        return total

    def tick(t, carry):
        group = group_of(s, t, segments)
        started = []

        def send(number, source, target, peer):
            copy = remote(source, target, send_sem.at[t, number], recv_sem.at[t, number], peer)
            copy.start()
            started.append(copy)

        def arrived(number, landing):
            remote(
                landing, landing, send_sem.at[t, number], recv_sem.at[t, number], after
            ).wait_recv()

        @pl.when(t > 0)
        def _():
            res_copy(t - 1).wait_recv()
            cur[t] = (res[t - 1].astype(F32) + landed(t - 1)).astype(BF16)

        values = cur[t].astype(F32)
        scale = lax.rsqrt(jnp.mean(values * values, axis=-1, keepdims=True) + EPSILON)
        xb[t, 0, 0] = (values * scale * gain_v[group]).astype(BF16)

        def gather_z(i):
            j = slot_from(ORDER[i])
            send(GZ + j, xb.at[t, 0, 0], xb.at[t, j, 0], at(s, 0, ORDER[i]))

        def gather_x(i):
            for off in range(1, NX):
                o = NX - off
                send(GX + i * 3 + o - 1, xb.at[t, i, 0], xb.at[t, i, o], at(s, off, 0))

        def gathered_x(i):
            for o in range(1, NX):
                arrived(GX + i * 3 + o - 1, xb.at[t, i, o])

        gather_z(1)
        gather_z(2)
        gather_x(0)
        for i in range(3, NZ):
            gather_z(i)

        @pl.when(t == 0)
        def _():
            for order in range(2):
                for i in range(3):
                    spare_copy(order, i, first_there).start()
            for i in range(1, NZ):
                coef_z(slot_from(ORDER[i]), at(s, 0, ORDER[i])).start()

        @pl.when(t < TICKS - 1)
        def _():
            res_copy(t).start()

        for i in range(1, NZ):
            arrived(GZ + i, xb.at[t, i, 0])
            gather_x(i)

        @pl.when(t == 0)
        def _():
            for j in range(1, NZ):
                coef_z(j, after).wait_recv()
            for off in range(1, NX):
                coef_x(NX - off, at(s, off, 0)).start()
            for load in loads[4:]:
                load.wait()
            for i in range(3):
                spare_copy(0, i, first_here).wait_recv()
            for o in range(1, NX):
                coef_x(o, after).wait_recv()

        @pl.when(t == 1)
        def _():
            for i in range(3):
                spare_copy(1, i, first_here).wait_recv()

        gate_w, up_w, down_w = flat(gw.at[group]), flat(uw.at[group]), flat(dw.at[group])
        contract = (((1,), (1,)), ((), ()))
        lanes = lax.broadcasted_iota(jnp.int32, (rows, LANES), 1)
        unit = lax.broadcasted_iota(jnp.int32, (rows, units), 1)
        base = t * 16

        for c in range(2):
            blocks = pl.ds(c * half, half)
            for i in range(c * half, c * half + half):
                gathered_x(i)
            normed = flat(xb.at[t, blocks])[...]
            gate = lax.dot_general(normed, gate_w[...], contract, preferred_element_type=F32)
            up = lax.dot_general(normed, up_w[...], contract, preferred_element_type=F32)
            factors = flat(coef.at[blocks])[...].astype(F32)

            def factor(which):
                spot = (lanes == base + which) | (lanes == base + which + 8)
                return jnp.sum(jnp.where(spot, factors, 0.0), axis=1, keepdims=True)

            scales = jnp.where(unit < home * tok, factor(x), factor(EXPERTS))
            hidden = gate / (1.0 + jnp.exp(-gate)) * up * scales
            hid[pl.ds(c * rows, rows)] = hidden.astype(BF16)

        for c in (1, 0):
            put(
                pb.at[pl.ds(c * half, half)],
                jnp.dot(
                    hid[pl.ds(c * rows, rows)], down_w[...], preferred_element_type=F32
                ).astype(BF16),
            )
            for i in range(c * half + half - 1, c * half - 1, -1):
                for off in range(1, NX):
                    o = NX - off
                    send(SX + i * 3 + o - 1, pb.at[i, off], rx.at[t, i, o - 1], at(s, off, 0))

        last = t == TICKS - 1
        to = jnp.where(last, s, s_after)
        for i in range(NZ - 1, -1, -1):
            for o in range(1, NX):
                arrived(SX + i * 3 + o - 1, rx.at[t, i, o - 1])
            total = pb[i, 0].astype(F32)
            for o in range(1, NX):
                total = total + rx[t, i, o - 1].astype(F32)
            sb[t, i] = total.astype(BF16)
            if i > 0:
                back_copy(t, i, at(to, 0, ORDER[i])).start()

        @pl.when(t < TICKS - 1)
        def _():
            back_copy(t, 0, after).start()

        @pl.when(last)
        def _():
            parts[t, 0] = sb[t, 0]

        for copy in started:
            copy.wait_send()

        return carry

    lax.fori_loop(0, TICKS, tick, 0)
    out[...] = (cur[TICKS - 1].astype(F32) + landed(TICKS - 1)).astype(BF16)
    for t in range(TICKS):
        for i in range(1, NZ):
            back_copy(t, i, after).wait_send()
        if t < TICKS - 1:
            back_copy(t, 0, after).wait_send()
            res_copy(t).wait_send()
    for i in range(3):
        for order in range(2):
            spare_copy(order, i, first_there).wait_send()
    for i in range(1, NZ):
        coef_z(i, after).wait_send()
    for o in range(1, NX):
        coef_x(o, after).wait_send()


def on_device(
    state, routes, gates, norm_gain, w_gate, w_up, w_down, spare_gate, spare_up, spare_down
):
    tok, width = state.shape[1:]
    home, extra = w_gate.shape[2], spare_gate.shape[2]
    units = -(-(home + extra) // 256) * 256

    def cut(weights):
        return weights.reshape(2, weights.shape[2] // tok, tok, width)

    vmem, hbm = pl.BlockSpec(memory_space=pltpu.VMEM), pl.BlockSpec(memory_space=pltpu.HBM)
    store = pltpu.VMEM((2, units // tok, tok, width), BF16)
    dma = pltpu.SemaphoreType.DMA
    final = pl.pallas_call(
        functools.partial(kernel, lax.axis_size("segment")),
        out_shape=jax.ShapeDtypeStruct((tok, width), BF16),
        in_specs=[hbm] * 10,
        out_specs=vmem,
        scratch_shapes=[
            pltpu.VMEM((TICKS, tok, width), BF16),
            pltpu.VMEM((TICKS, 2, tok), jnp.int32),
            pltpu.VMEM((TICKS, 2, tok), F32),
            pltpu.VMEM((2, 1, width), F32),
            pltpu.VMEM((NZ, NX, tok, LANES), BF16),
            store,
            store,
            store,
            pltpu.VMEM((TICKS, NZ, NX, tok, width), BF16),
            pltpu.VMEM((NZ * NX * tok, units), BF16),
            pltpu.VMEM((NZ, NX, tok, width), BF16),
            pltpu.VMEM((TICKS, NZ, NX - 1, tok, width), BF16),
            pltpu.VMEM((TICKS, NZ, tok, width), BF16),
            pltpu.VMEM((TICKS - 1, tok, width), BF16),
            pltpu.VMEM((TICKS, NZ, tok, width), BF16),
            dma((TICKS, COPIES)),
            dma((TICKS, COPIES)),
            dma((TICKS - 1,)),
            dma((TICKS - 1,)),
            dma((7,)),
            dma((2, 3)),
            dma((2, 3)),
            dma((NZ + NX - 1,)),
            dma((NZ + NX - 1,)),
        ],
        compiler_params=pltpu.CompilerParams(
            collective_id=0, has_side_effects=True, vmem_limit_bytes=60 * 1024 * 1024
        ),
    )(
        state[0],
        jnp.swapaxes(routes[:, 0], 1, 2),
        jnp.swapaxes(gates[:, 0], 1, 2),
        norm_gain,
        cut(w_gate),
        cut(w_up),
        cut(w_down),
        cut(spare_gate),
        cut(spare_up),
        cut(spare_down),
    )
    return final[None]


def solution(mesh):
    return jax.shard_map(
        on_device,
        mesh=mesh,
        in_specs=(
            P("segment", "expert", None),
            P(None, "segment", "expert", None),
            P(None, "segment", "expert", None),
            P(None, "segment", None),
            P(None, "segment", "expert", None),
            P(None, "segment", "expert", None),
            P(None, "segment", "expert", None),
            P(None, "segment", "expert", None),
            P(None, "segment", "expert", None),
            P(None, "segment", "expert", None),
        ),
        out_specs=P("segment", "expert", None),
        check_vma=False,
    )
```

time: 475 us -> 152 us (0.32)
  the two profiles are of different devices: /device:TPU:1 before, /device:TPU:24 now
where the time goes in v2:
time: 152 us
  Pallas kernels  151 us (99%)
    pallas_call x1, Pallas kernels, on_device(): pl.pallas_call(functools.partial(kernel, lax.axis_size('segment')), out_s...  151 us

profile of v2, /device:TPU:24, one launch (start us, length us, event | category | flops | bytes accessed | tf_op | source)
XLA Modules:
  0.0 152.3 jit_solution(9326421662655237457)
XLA Ops:
  0.0 150.9 %shard_map.100 = bf16[8,2048]{1,0:T(8,128)(2,1)} custom-call(bf16[8,2048]{1,0:T(8,128)(2,1)} %bitcast.21, s32[4,2,8]{2,1,0:T(2,128)} %bitcast.22, f32[4,2,8]{2,1,0:T(2,128)} %bitcast.23, f32[2,1,2048]{2,1,0:T(1,128)} %gain.1, bf16[2,20,8,2048]{3,2,1,0:T(8,128)(2,1)} %bitcast.14, bf16[2,20,8,2048]{3,2,1,0:T(8,128)(2,1)} %bitcast.15, ...), custom_call_target="tpu_custom_call" | custom-call | tf_op jit(solution)/shard_map/pallas_call | solution.py:344
  150.9 1.4 copy.18

commit v3 on v2

--- a/solution.py
+++ b/solution.py
@@ -24,10 +24,15 @@
     return first + jnp.where(start + tick_idx >= segments, 1, 0)
 
 
-ORDER = (0, 1, -1, 2, -2, 3, -3, 4)
+ORDER = (0, 4, 3, -3, 2, -2, 1, -1)
 NZ, NX = 8, 4
-GZ, GX, SX, SZ = 0, 8, 32, 56
-COPIES = 64
+X_FIRST = 512
+X_LAST = 512
+GX, SX, GZ, GAX, GAZ, SAZ = 0, 8, 16, 24, 25, 27
+GROUPS = 28
+SENT_GZ, SENT_GX, SENT_GAX, SENT_GAZ, SENT_SX, SENT_SAZ = range(6)
+BACK = (1, 2, 3, 0, 4, 5, 6, 7)
+A_AFTER = 5
 
 
 def slot_from(offset):
@@ -46,12 +51,14 @@
     segments,
     state, routes, gates, gain, w_gate, w_up, w_down, spare_g, spare_u, spare_d,
     out,
-    cur, routes_v, gates_v, gain_v, coef, gw, uw, dw, xb, hid, pb, rx, sb, res, parts,
-    send_sem, recv_sem, res_send, res_recv, w_sem, spare_send, spare_recv, coef_send, coef_recv,
+    cur, routes_v, gates_v, gain_v, coef, gw, uw, dw, xa, xb, hid, pa, pb, ra, rx, sa, sb, res,
+    parts_a, parts_b,
+    send_sem, recv_sem, back_send, back_recv, res_send, res_recv, w_sem, spare_send, spare_recv, coef_send, coef_recv,
 ):
     tok, width = state.shape
     home, extra = w_gate.shape[1], spare_g.shape[1]
     units = gw.shape[1] * tok
+    aw, lw = xa.shape[-1], pa.shape[-1]
     half = NZ // 2
     rows = half * NX * tok
     s = lax.axis_index("segment")
@@ -86,6 +93,7 @@
     peers += [at(s, 0, off) for off in range(1, NZ)]
     for section in (s_after, s_before):
         peers += [at(section, 0, off) for off in range(NZ)]
+        peers += [at(section, off, 0) for off in range(1, NX)]
     for peer in peers:
         pl.semaphore_signal(barrier, inc=1, device_id=peer, device_id_type=MESH)
 
@@ -146,71 +154,100 @@
         )
 
     def coef_z(j, peer):
-        return remote(coef.at[0, 0], coef.at[j, 0], coef_send.at[j], coef_recv.at[j], peer)
+        return remote(coef.at[0, 0], coef.at[j, 0], coef_send.at[0], coef_recv.at[0], peer)
 
     def coef_x(o, peer):
-        n = NZ - 1 + o
-        return remote(coef.at[:, 0], coef.at[:, o], coef_send.at[n], coef_recv.at[n], peer)
+        return remote(coef.at[:, 0], coef.at[:, o], coef_send.at[1], coef_recv.at[1], peer)
+
+    def group(ref, sent, got):
+        return remote(ref, ref, sent, got, after)
+
+    coefs_z = group(coef.at[pl.ds(1, NZ - 1), 0], coef_send.at[0], coef_recv.at[0])
+    coefs_x = group(coef.at[:, pl.ds(1, NX - 1)], coef_send.at[1], coef_recv.at[1])
 
     def res_copy(t):
         return remote(cur.at[t], res.at[t], res_send.at[t], res_recv.at[t], after)
 
-    def back_copy(t, i, peer):
-        j = slot_from(ORDER[i])
-        n = SZ + j
-        return remote(sb.at[t, i], parts.at[t, j], send_sem.at[t, n], recv_sem.at[t, n], peer)
+    def back_sem(t, i, first):
+        n = first if i > 0 else first + 2
+        return back_send.at[t, n], back_recv.at[t, n]
+
+    def back_b(t, i, peer):
+        return remote(sb.at[t, i], parts_b.at[t, slot_from(ORDER[i])], *back_sem(t, i, 0), peer)
+
+    def back_a(t, off, peer):
+        o = (NX - off) % NX
+        return remote(sa.at[t, off], parts_a.at[t, o], *back_sem(t, off, 1), peer)
+
+    def back_groups(t):
+        return (
+            group(parts_b.at[t, pl.ds(1, NZ - 1)], *back_sem(t, 1, 0)),
+            group(parts_a.at[t, pl.ds(1, NX - 1)], *back_sem(t, 1, 1)),
+        )
+
+    def back_own(t):
+        return back_b(t, 0, after), back_a(t, 0, after)
 
     def landed(t):
-        for j in range(NZ - 1, -1, -1):
-            target = parts.at[t, j]
-            n = SZ + j
-            if j == 0:
-                @pl.when(t < TICKS - 1)
-                def _():
-                    remote(target, target, send_sem.at[t, n], recv_sem.at[t, n], after).wait_recv()
-            else:
-                remote(target, target, send_sem.at[t, n], recv_sem.at[t, n], after).wait_recv()
-        total = parts[t, NZ - 1].astype(F32)
-        for j in range(NZ - 2, -1, -1):
-            total = total + parts[t, j].astype(F32)
-        return total
+        for copies in back_groups(t):
+            copies.wait_recv()
+
+        @pl.when(t < TICKS - 1)
+        def _():
+            for copy in back_own(t):
+                copy.wait_recv()
+
+        sums = []
+        for parts, count in ((parts_a, NX), (parts_b, NZ)):
+            total = parts[t, 0].astype(F32)
+            for j in range(1, count):
+                total = total + parts[t, j].astype(F32)
+            sums.append(total)
+        return sums
+
+    def next_state(base, t):
+        sum_a, sum_b = landed(t)
+        base = base.astype(F32)
+        return (base[:, :lw] + sum_a).astype(BF16), (base[:, lw:] + sum_b).astype(BF16)
 
     def tick(t, carry):
-        group = group_of(s, t, segments)
-        started = []
-
-        def send(number, source, target, peer):
-            copy = remote(source, target, send_sem.at[t, number], recv_sem.at[t, number], peer)
-            copy.start()
-            started.append(copy)
-
-        def arrived(number, landing):
-            remote(
-                landing, landing, send_sem.at[t, number], recv_sem.at[t, number], after
-            ).wait_recv()
+        layer = group_of(s, t, segments)
+
+        def send(sent, got, source, target, peer):
+            remote(source, target, send_sem.at[sent], recv_sem.at[got], peer).start()
+
+        def arrived(got, landing):
+            group(landing, send_sem.at[0], recv_sem.at[got]).wait_recv()
+
+        def left(sent, shape_of):
+            group(shape_of, send_sem.at[sent], recv_sem.at[0]).wait_send()
 
         @pl.when(t > 0)
         def _():
             res_copy(t - 1).wait_recv()
-            cur[t] = (res[t - 1].astype(F32) + landed(t - 1)).astype(BF16)
+            cur[t, :, :lw], cur[t, :, lw:] = next_state(res[t - 1], t - 1)
 
         values = cur[t].astype(F32)
         scale = lax.rsqrt(jnp.mean(values * values, axis=-1, keepdims=True) + EPSILON)
-        xb[t, 0, 0] = (values * scale * gain_v[group]).astype(BF16)
+        normed = (values * scale * gain_v[layer]).astype(BF16)
+        xa[t, 0, 0] = normed[:, :aw]
+        xb[t, 0, 0] = normed[:, aw:]
 
         def gather_z(i):
             j = slot_from(ORDER[i])
-            send(GZ + j, xb.at[t, 0, 0], xb.at[t, j, 0], at(s, 0, ORDER[i]))
+            send(SENT_GZ, GZ + j, xb.at[t, 0, 0], xb.at[t, j, 0], at(s, 0, ORDER[i]))
 
         def gather_x(i):
             for off in range(1, NX):
                 o = NX - off
-                send(GX + i * 3 + o - 1, xb.at[t, i, 0], xb.at[t, i, o], at(s, off, 0))
+                send(SENT_GX, GX + i, xb.at[t, i, 0], xb.at[t, i, o], at(s, off, 0))
 
         def gathered_x(i):
-            for o in range(1, NX):
-                arrived(GX + i * 3 + o - 1, xb.at[t, i, o])
-
+            arrived(GX + i, xb.at[t, i, pl.ds(1, NX - 1)])
+
+        for off in range(1, NX):
+            o = NX - off
+            send(SENT_GAX, GAX, xa.at[t, 0, 0], xa.at[t, 0, o], at(s, off, 0))
         gather_z(1)
         gather_z(2)
         gather_x(0)
@@ -232,26 +269,29 @@
         for i in range(1, NZ):
             arrived(GZ + i, xb.at[t, i, 0])
             gather_x(i)
+            if i == 2:
+                arrived(GAX, xa.at[t, 0, pl.ds(1, NX - 1)])
+                for k in range(1, NZ):
+                    j = slot_from(ORDER[k])
+                    send(SENT_GAZ, GAZ + j // half, xa.at[t, 0], xa.at[t, j], at(s, 0, ORDER[k]))
 
         @pl.when(t == 0)
         def _():
-            for j in range(1, NZ):
-                coef_z(j, after).wait_recv()
+            coefs_z.wait_recv()
             for off in range(1, NX):
                 coef_x(NX - off, at(s, off, 0)).start()
             for load in loads[4:]:
                 load.wait()
             for i in range(3):
                 spare_copy(0, i, first_here).wait_recv()
-            for o in range(1, NX):
-                coef_x(o, after).wait_recv()
+            coefs_x.wait_recv()
 
         @pl.when(t == 1)
         def _():
             for i in range(3):
                 spare_copy(1, i, first_here).wait_recv()
 
-        gate_w, up_w, down_w = flat(gw.at[group]), flat(uw.at[group]), flat(dw.at[group])
+        gate_w, up_w, down_w = flat(gw.at[layer]), flat(uw.at[layer]), flat(dw.at[layer])
         contract = (((1,), (1,)), ((), ()))
         lanes = lax.broadcasted_iota(jnp.int32, (rows, LANES), 1)
         unit = lax.broadcasted_iota(jnp.int32, (rows, units), 1)
@@ -261,9 +301,17 @@
             blocks = pl.ds(c * half, half)
             for i in range(c * half, c * half + half):
                 gathered_x(i)
-            normed = flat(xb.at[t, blocks])[...]
-            gate = lax.dot_general(normed, gate_w[...], contract, preferred_element_type=F32)
-            up = lax.dot_general(normed, up_w[...], contract, preferred_element_type=F32)
+            arrived(GAZ + c, xa.at[t, pl.ds(c * half + 1 - c, half - 1 + c)])
+            rows_a, rows_b = flat(xa.at[t, blocks])[...], flat(xb.at[t, blocks])[...]
+
+            def product(weight):
+                return lax.dot_general(
+                    rows_a, weight[:, :aw], contract, preferred_element_type=F32
+                ) + lax.dot_general(
+                    rows_b, weight[:, aw:], contract, preferred_element_type=F32
+                )
+
+            gate, up = product(gate_w), product(up_w)
             factors = flat(coef.at[blocks])[...].astype(F32)
 
             def factor(which):
@@ -274,58 +322,76 @@
             hidden = gate / (1.0 + jnp.exp(-gate)) * up * scales
             hid[pl.ds(c * rows, rows)] = hidden.astype(BF16)
 
-        for c in (1, 0):
-            put(
-                pb.at[pl.ds(c * half, half)],
-                jnp.dot(
-                    hid[pl.ds(c * rows, rows)], down_w[...], preferred_element_type=F32
-                ).astype(BF16),
-            )
-            for i in range(c * half + half - 1, c * half - 1, -1):
+
+            for part, columns in ((pb, slice(lw, width)), (pa, slice(0, lw))):
+                put(
+                    part.at[blocks],
+                    jnp.dot(
+                        hid[pl.ds(c * rows, rows)],
+                        down_w[:, columns],
+                        preferred_element_type=F32,
+                    ).astype(BF16),
+                )
+            for i in range(c * half, c * half + half):
                 for off in range(1, NX):
                     o = NX - off
-                    send(SX + i * 3 + o - 1, pb.at[i, off], rx.at[t, i, o - 1], at(s, off, 0))
+                    send(SENT_SX, SX + i, pb.at[i, off], rx.at[t, i, o - 1], at(s, off, 0))
+                if i > 0:
+                    j = slot_from(ORDER[i])
+                    send(SENT_SAZ, SAZ, pa.at[i], ra.at[t, j], at(s, 0, ORDER[i]))
 
         last = t == TICKS - 1
         to = jnp.where(last, s, s_after)
-        for i in range(NZ - 1, -1, -1):
-            for o in range(1, NX):
-                arrived(SX + i * 3 + o - 1, rx.at[t, i, o - 1])
+        for i in BACK:
+            arrived(SX + i, rx.at[t, i])
             total = pb[i, 0].astype(F32)
             for o in range(1, NX):
                 total = total + rx[t, i, o - 1].astype(F32)
             sb[t, i] = total.astype(BF16)
             if i > 0:
-                back_copy(t, i, at(to, 0, ORDER[i])).start()
+                back_b(t, i, at(to, 0, ORDER[i])).start()
+            if i == A_AFTER:
+                arrived(SAZ, ra.at[t, pl.ds(1, NZ - 1)])
+                total = pa[0].astype(F32)
+                for j in range(1, NZ):
+                    total = total + ra[t, j].astype(F32)
+                sa[t] = total.astype(BF16)
+                for off in range(1, NX):
+                    back_a(t, off, at(to, off, 0)).start()
 
         @pl.when(t < TICKS - 1)
         def _():
-            back_copy(t, 0, after).start()
+            for copy in back_own(t):
+                copy.start()
 
         @pl.when(last)
         def _():
-            parts[t, 0] = sb[t, 0]
-
-        for copy in started:
-            copy.wait_send()
+            parts_b[t, 0] = sb[t, 0]
+            parts_a[t, 0] = sa[t, 0]
+
+        left(SENT_GZ, xb.at[t, pl.ds(1, NZ - 1), 0])
+        left(SENT_GX, xb.at[t, :, pl.ds(1, NX - 1)])
+        left(SENT_GAX, xa.at[t, 0, pl.ds(1, NX - 1)])
+        left(SENT_GAZ, xa.at[t, pl.ds(1, NZ - 1)])
+        left(SENT_SX, rx.at[t])
+        left(SENT_SAZ, ra.at[t, pl.ds(1, NZ - 1)])
 
         return carry
 
     lax.fori_loop(0, TICKS, tick, 0)
-    out[...] = (cur[TICKS - 1].astype(F32) + landed(TICKS - 1)).astype(BF16)
+    out[:, :lw], out[:, lw:] = next_state(cur[TICKS - 1], TICKS - 1)
     for t in range(TICKS):
-        for i in range(1, NZ):
-            back_copy(t, i, after).wait_send()
+        for copies in back_groups(t):
+            copies.wait_send()
         if t < TICKS - 1:
-            back_copy(t, 0, after).wait_send()
+            for copy in back_own(t):
+                copy.wait_send()
             res_copy(t).wait_send()
     for i in range(3):
         for order in range(2):
             spare_copy(order, i, first_there).wait_send()
-    for i in range(1, NZ):
-        coef_z(i, after).wait_send()
-    for o in range(1, NX):
-        coef_x(o, after).wait_send()
+    coefs_z.wait_send()
+    coefs_x.wait_send()
 
 
 def on_device(
@@ -334,6 +400,10 @@
     tok, width = state.shape[1:]
     home, extra = w_gate.shape[2], spare_gate.shape[2]
     units = -(-(home + extra) // 256) * 256
+    aw = min(X_FIRST, width // 2)
+    bw = width - aw
+    lw = min(X_LAST, width // 2)
+    rw = width - lw
 
     def cut(weights):
         return weights.reshape(2, weights.shape[2] // tok, tok, width)
@@ -355,22 +425,29 @@
             store,
             store,
             store,
-            pltpu.VMEM((TICKS, NZ, NX, tok, width), BF16),
+            pltpu.VMEM((TICKS, NZ, NX, tok, aw), BF16),
+            pltpu.VMEM((TICKS, NZ, NX, tok, bw), BF16),
             pltpu.VMEM((NZ * NX * tok, units), BF16),
-            pltpu.VMEM((NZ, NX, tok, width), BF16),
-            pltpu.VMEM((TICKS, NZ, NX - 1, tok, width), BF16),
-            pltpu.VMEM((TICKS, NZ, tok, width), BF16),
+            pltpu.VMEM((NZ, NX, tok, lw), BF16),
+            pltpu.VMEM((NZ, NX, tok, rw), BF16),
+            pltpu.VMEM((TICKS, NZ, NX, tok, lw), BF16),
+            pltpu.VMEM((TICKS, NZ, NX - 1, tok, rw), BF16),
+            pltpu.VMEM((TICKS, NX, tok, lw), BF16),
+            pltpu.VMEM((TICKS, NZ, tok, rw), BF16),
             pltpu.VMEM((TICKS - 1, tok, width), BF16),
-            pltpu.VMEM((TICKS, NZ, tok, width), BF16),
-            dma((TICKS, COPIES)),
-            dma((TICKS, COPIES)),
+            pltpu.VMEM((TICKS, NX, tok, lw), BF16),
+            pltpu.VMEM((TICKS, NZ, tok, rw), BF16),
+            dma((6,)),
+            dma((GROUPS,)),
+            dma((TICKS, 4)),
+            dma((TICKS, 4)),
             dma((TICKS - 1,)),
             dma((TICKS - 1,)),
             dma((7,)),
             dma((2, 3)),
             dma((2, 3)),
-            dma((NZ + NX - 1,)),
-            dma((NZ + NX - 1,)),
+            dma((2,)),
+            dma((2,)),
         ],
         compiler_params=pltpu.CompilerParams(
             collective_id=0, has_side_effects=True, vmem_limit_bytes=60 * 1024 * 1024

time: 152 us -> 128 us (0.84)
  the two profiles are of different devices: /device:TPU:24 before, /device:TPU:1 now
where the time goes in v3:
time: 128 us
  Pallas kernels  126 us (98%)
  local copies, waits for them, and re-layouts  1.38 us (1%)
    pallas_call x1, Pallas kernels, on_device(): pl.pallas_call(functools.partial(kernel, lax.axis_size('segment')), out_s...  126 us

profile of v3, /device:TPU:1, one launch (start us, length us, event | category | flops | bytes accessed | tf_op | source)
XLA Modules:
  0.0 127.6 jit_solution(3611726709694487370)
XLA Ops:
  0.0 126.2 %shard_map.100 = bf16[8,2048]{1,0:T(8,128)(2,1)} custom-call(bf16[8,2048]{1,0:T(8,128)(2,1)} %bitcast.21, s32[4,2,8]{2,1,0:T(2,128)} %bitcast.22, f32[4,2,8]{2,1,0:T(2,128)} %bitcast.23, f32[2,1,2048]{2,1,0:T(1,128)} %gain.1, bf16[2,20,8,2048]{3,2,1,0:T(8,128)(2,1)} %bitcast.14, bf16[2,20,8,2048]{3,2,1,0:T(8,128)(2,1)} %bitcast.15, ...), custom_call_target="tpu_custom_call" | custom-call | tf_op jit(solution)/shard_map/pallas_call | solution.py:414
  126.2 1.4 %copy.18 = bf16[1,8,2048]{2,1,0:T(8,128)(2,1)} copy(bf16[1,8,2048]{2,1,0:T(8,128)(2,1)} %bitcast.20) | data formatting | bytes 65536

commit v4 on v3

--- a/solution.py
+++ b/solution.py
@@ -24,19 +24,24 @@
     return first + jnp.where(start + tick_idx >= segments, 1, 0)
 
 
-ORDER = (0, 4, 3, -3, 2, -2, 1, -1)
+ORDER = (0, 1, -1, 4, 3, -3, 2, -2)
 NZ, NX = 8, 4
 X_FIRST = 512
 X_LAST = 512
-GX, SX, GZ, GAX, GAZ, SAZ = 0, 8, 16, 24, 25, 27
-GROUPS = 28
+GX, SX, GZ, GAX, SAZ, GAZ = 0, 8, 16, 24, 25, 26
+CHUNKS = ((0, 3), (3, 6), (6, 8))
+GROUPS = GAZ + len(CHUNKS)
 SENT_GZ, SENT_GX, SENT_GAX, SENT_GAZ, SENT_SX, SENT_SAZ = range(6)
-BACK = (1, 2, 3, 0, 4, 5, 6, 7)
+BACK = (1, 2, 0, 3, 4, 5, 6, 7)
 A_AFTER = 5
 
 
 def slot_from(offset):
     return next(i for i, d in enumerate(ORDER) if (d + offset) % NZ == 0)
+
+
+def chunk_of(slot):
+    return next(c for c, (low, high) in enumerate(CHUNKS) if low <= slot < high)
 
 
 def flat(ref):
@@ -59,8 +64,6 @@
     home, extra = w_gate.shape[1], spare_g.shape[1]
     units = gw.shape[1] * tok
     aw, lw = xa.shape[-1], pa.shape[-1]
-    half = NZ // 2
-    rows = half * NX * tok
     s = lax.axis_index("segment")
     mine = lax.axis_index("expert")
     x, z = mine // NZ, lax.rem(mine, NZ)
@@ -245,6 +248,11 @@
         def gathered_x(i):
             arrived(GX + i, xb.at[t, i, pl.ds(1, NX - 1)])
 
+        @pl.when(t == 0)
+        def _():
+            for i in range(1, NZ):
+                coef_z(slot_from(ORDER[i]), at(s, 0, ORDER[i])).start()
+
         for off in range(1, NX):
             o = NX - off
             send(SENT_GAX, GAX, xa.at[t, 0, 0], xa.at[t, 0, o], at(s, off, 0))
@@ -259,8 +267,6 @@
             for order in range(2):
                 for i in range(3):
                     spare_copy(order, i, first_there).start()
-            for i in range(1, NZ):
-                coef_z(slot_from(ORDER[i]), at(s, 0, ORDER[i])).start()
 
         @pl.when(t < TICKS - 1)
         def _():
@@ -270,16 +276,19 @@
             arrived(GZ + i, xb.at[t, i, 0])
             gather_x(i)
             if i == 2:
+                @pl.when(t == 0)
+                def _():
+                    coefs_z.wait_recv()
+                    for off in range(1, NX):
+                        coef_x(NX - off, at(s, off, 0)).start()
+
                 arrived(GAX, xa.at[t, 0, pl.ds(1, NX - 1)])
-                for k in range(1, NZ):
+                for k in (3, 4, 5, 1, 2, 6, 7):
                     j = slot_from(ORDER[k])
-                    send(SENT_GAZ, GAZ + j // half, xa.at[t, 0], xa.at[t, j], at(s, 0, ORDER[k]))
+                    send(SENT_GAZ, GAZ + chunk_of(j), xa.at[t, 0], xa.at[t, j], at(s, 0, ORDER[k]))
 
         @pl.when(t == 0)
         def _():
-            coefs_z.wait_recv()
-            for off in range(1, NX):
-                coef_x(NX - off, at(s, off, 0)).start()
             for load in loads[4:]:
                 load.wait()
             for i in range(3):
@@ -293,25 +302,39 @@
 
         gate_w, up_w, down_w = flat(gw.at[layer]), flat(uw.at[layer]), flat(dw.at[layer])
         contract = (((1,), (1,)), ((), ()))
-        lanes = lax.broadcasted_iota(jnp.int32, (rows, LANES), 1)
-        unit = lax.broadcasted_iota(jnp.int32, (rows, units), 1)
         base = t * 16
 
-        for c in range(2):
-            blocks = pl.ds(c * half, half)
-            for i in range(c * half, c * half + half):
-                gathered_x(i)
-            arrived(GAZ + c, xa.at[t, pl.ds(c * half + 1 - c, half - 1 + c)])
-            rows_a, rows_b = flat(xa.at[t, blocks])[...], flat(xb.at[t, blocks])[...]
-
-            def product(weight):
-                return lax.dot_general(
-                    rows_a, weight[:, :aw], contract, preferred_element_type=F32
-                ) + lax.dot_general(
-                    rows_b, weight[:, aw:], contract, preferred_element_type=F32
+        for c, (low, high) in enumerate(CHUNKS):
+            blocks = pl.ds(low, high - low)
+            rows = (high - low) * NX * tok
+            span = pl.ds(low * NX * tok, rows)
+            others = range(max(low, 1), high)
+            lanes = lax.broadcasted_iota(jnp.int32, (rows, LANES), 1)
+            unit = lax.broadcasted_iota(jnp.int32, (rows, units), 1)
+
+            def product(ref, columns):
+                values = flat(ref.at[t, blocks])[...]
+                return tuple(
+                    lax.dot_general(
+                        values, weight[:, columns], contract, preferred_element_type=F32
+                    )
+                    for weight in (gate_w, up_w)
                 )
 
-            gate, up = product(gate_w), product(up_w)
+            def part_a():
+                arrived(GAZ + c, xa.at[t, pl.ds(others[0], len(others))])
+                return product(xa, slice(0, aw))
+
+            def part_b():
+                for i in range(low, high):
+                    gathered_x(i)
+                return product(xb, slice(aw, width))
+
+            if c == 0:
+                (gate_b, up_b), (gate_a, up_a) = part_b(), part_a()
+            else:
+                (gate_a, up_a), (gate_b, up_b) = part_a(), part_b()
+            gate, up = gate_a + gate_b, up_a + up_b
             factors = flat(coef.at[blocks])[...].astype(F32)
 
             def factor(which):
@@ -320,25 +343,23 @@
 
             scales = jnp.where(unit < home * tok, factor(x), factor(EXPERTS))
             hidden = gate / (1.0 + jnp.exp(-gate)) * up * scales
-            hid[pl.ds(c * rows, rows)] = hidden.astype(BF16)
-
-
-            for part, columns in ((pb, slice(lw, width)), (pa, slice(0, lw))):
-                put(
-                    part.at[blocks],
-                    jnp.dot(
-                        hid[pl.ds(c * rows, rows)],
-                        down_w[:, columns],
-                        preferred_element_type=F32,
-                    ).astype(BF16),
-                )
-            for i in range(c * half, c * half + half):
+            hid[span] = hidden.astype(BF16)
+
+
+            done = hid[span]
+
+            def down(part, columns):
+                value = jnp.dot(done, down_w[:, columns], preferred_element_type=F32)
+                put(part.at[blocks], value.astype(BF16))
+
+            down(pb, slice(lw, width))
+            for i in sorted(range(low, high), key=BACK.index):
                 for off in range(1, NX):
-                    o = NX - off
-                    send(SENT_SX, SX + i, pb.at[i, off], rx.at[t, i, o - 1], at(s, off, 0))
-                if i > 0:
-                    j = slot_from(ORDER[i])
-                    send(SENT_SAZ, SAZ, pa.at[i], ra.at[t, j], at(s, 0, ORDER[i]))
+                    send(SENT_SX, SX + i, pb.at[i, off], rx.at[t, i, NX - off - 1], at(s, off, 0))
+            down(pa, slice(0, lw))
+            for i in others:
+                j = slot_from(ORDER[i])
+                send(SENT_SAZ, SAZ, pa.at[i], ra.at[t, j], at(s, 0, ORDER[i]))
 
         last = t == TICKS - 1
         to = jnp.where(last, s, s_after)

time: 128 us -> 123 us (0.961)
  Pallas kernels: 126 us -> 122 us
    pallas_call x1, Pallas kernels: 126 us -> 122 us  [on_device(): pl.pallas_call(functools.partial(kernel, lax.axis_size('segment')), out_s...]
where the time goes in v4:
time: 123 us
  Pallas kernels  122 us (99%)
  local copies, waits for them, and re-layouts  1.38 us (1%)
    pallas_call x1, Pallas kernels, on_device(): pl.pallas_call(functools.partial(kernel, lax.axis_size('segment')), out_s...  122 us

profile of v4, /device:TPU:1, one launch (start us, length us, event | category | flops | bytes accessed | tf_op | source)
XLA Modules:
  0.0 122.9 jit_solution(114037482998122509)
XLA Ops:
  0.0 121.5 %shard_map.100 = bf16[8,2048]{1,0:T(8,128)(2,1)} custom-call(bf16[8,2048]{1,0:T(8,128)(2,1)} %bitcast.21, s32[4,2,8]{2,1,0:T(2,128)} %bitcast.22, f32[4,2,8]{2,1,0:T(2,128)} %bitcast.23, f32[2,1,2048]{2,1,0:T(1,128)} %gain.1, bf16[2,20,8,2048]{3,2,1,0:T(8,128)(2,1)} %bitcast.14, bf16[2,20,8,2048]{3,2,1,0:T(8,128)(2,1)} %bitcast.15, ...), custom_call_target="tpu_custom_call" | custom-call | tf_op jit(solution)/shard_map/pallas_call | solution.py:435
  121.5 1.4 %copy.18 = bf16[1,8,2048]{2,1,0:T(8,128)(2,1)} copy(bf16[1,8,2048]{2,1,0:T(8,128)(2,1)} %bitcast.20) | data formatting | bytes 65536

commit v5 on v4

--- a/solution.py
+++ b/solution.py
@@ -29,10 +29,10 @@
 X_FIRST = 512
 X_LAST = 512
 GX, SX, GZ, GAX, SAZ, GAZ = 0, 8, 16, 24, 25, 26
-CHUNKS = ((0, 3), (3, 6), (6, 8))
+CHUNKS = ((0, 4), (4, 6), (6, 8))
 GROUPS = GAZ + len(CHUNKS)
 SENT_GZ, SENT_GX, SENT_GAX, SENT_GAZ, SENT_SX, SENT_SAZ = range(6)
-BACK = (1, 2, 0, 3, 4, 5, 6, 7)
+BACK = (1, 2, 3, 4, 5, 6, 7, 0)
 A_AFTER = 5
 
 
@@ -353,7 +353,7 @@
                 put(part.at[blocks], value.astype(BF16))
 
             down(pb, slice(lw, width))
-            for i in sorted(range(low, high), key=BACK.index):
+            for i in (*others, 0) if high == NZ else others:
                 for off in range(1, NX):
                     send(SENT_SX, SX + i, pb.at[i, off], rx.at[t, i, NX - off - 1], at(s, off, 0))
             down(pa, slice(0, lw))

time: 123 us -> 120 us (0.976)
  Pallas kernels: 122 us -> 118 us
    pallas_call x1, Pallas kernels: 122 us -> 118 us  [on_device(): pl.pallas_call(functools.partial(kernel, lax.axis_size('segment')), out_s...]
where the time goes in v5:
time: 120 us; the launch traced here: 119 us
  Pallas kernels  118 us (98%)
  local copies, waits for them, and re-layouts  1.38 us (1%)
    pallas_call x1, Pallas kernels, on_device(): pl.pallas_call(functools.partial(kernel, lax.axis_size('segment')), out_s...  118 us

profile of v5, /device:TPU:1, one launch (start us, length us, event | category | flops | bytes accessed | tf_op | source)
XLA Modules:
  0.0 119.2 jit_solution(1709770194440088237)
XLA Ops:
  0.0 117.8 %shard_map.100 = bf16[8,2048]{1,0:T(8,128)(2,1)} custom-call(bf16[8,2048]{1,0:T(8,128)(2,1)} %bitcast.21, s32[4,2,8]{2,1,0:T(2,128)} %bitcast.22, f32[4,2,8]{2,1,0:T(2,128)} %bitcast.23, f32[2,1,2048]{2,1,0:T(1,128)} %gain.1, bf16[2,20,8,2048]{3,2,1,0:T(8,128)(2,1)} %bitcast.14, bf16[2,20,8,2048]{3,2,1,0:T(8,128)(2,1)} %bitcast.15, ...), custom_call_target="tpu_custom_call" | custom-call | tf_op jit(solution)/shard_map/pallas_call | solution.py:435
  117.8 1.4 %copy.18 = bf16[1,8,2048]{2,1,0:T(8,128)(2,1)} copy(bf16[1,8,2048]{2,1,0:T(8,128)(2,1)} %bitcast.20) | data formatting | bytes 65536
